TPU v7x, 256 devices: a whole 4x4x8 slice. The times are simulated.
256 devices in a mesh: member: 4 (over z_lo), lat: 64 (over z_hi, y, x, core).
Axes of the slice: x: 4, y: 4, z: 8 (z_hi: 2, z_lo: 4; z = z_hi * 4 + z_lo), core: 2. Of those that a mesh axis runs over, the one named last changes fastest.
Arguments:
- grid_input: bfloat16 [4, 384, 768, 256], P('member', 'lat'), may hold values from -6 to 6
- saved_mixed: bfloat16 [4, 384, 768, 256], P('member', 'lat'), may hold values from -6 to 6
- target: bfloat16 [384, 768, 256], P('lat'), may hold values from -6 to 6
- land_weight: int32 [384, 768], P('lat'), may hold values from 0 to 3
- mix_weight: bfloat16 [256, 256], replicated, may hold values from -0.375 to 0.375
- degree_gain: float32 [384], replicated, may hold values from 0.3 to 3
- up_weight: bfloat16 [256, 512], replicated, may hold values from -0.375 to 0.375
- down_weight: bfloat16 [512, 256], replicated, may hold values from -0.25 to 0.25
Outputs:
- grad_input: bfloat16 [4, 384, 768, 256], P('member', 'lat')
All inputs are finite; a program needn't handle non-finite values.
Results may differ from a plain program's by a relative error of at most 0.015.
Values may be sent and summed in bfloat16 or wider, within the bound.
A program may use at most 128 MiB of HBM per device.

v0:
```python
import math

import jax
import jax.numpy as jnp
from jax import lax
from jax.sharding import PartitionSpec as P

kappa_gelu = 0.7978845608
cubic_gelu = 0.044715
smooth_square = 0.25


def gelu_parts(inputs):
    tanh_part = jnp.tanh(kappa_gelu * (inputs + cubic_gelu * inputs * inputs * inputs))
    values = 0.5 * inputs * (1.0 + tanh_part)
    slopes = 0.5 * (1.0 + tanh_part) + 0.5 * inputs * (1.0 - tanh_part * tanh_part) * kappa_gelu * (
        1.0 + 3.0 * cubic_gelu * inputs * inputs
    )
    return (values, slopes)


def slope_abs(difference):
    return difference * lax.rsqrt(difference * difference + smooth_square)


def member_term(own_values, everyone, target, weights):
    member_count = everyone.shape[0]
    total = jnp.zeros(own_values.shape, jnp.float32)
    for slot in range(member_count):
        total = total + slope_abs(own_values - everyone[slot].astype(jnp.float32))
    direct = slope_abs(own_values - target.astype(jnp.float32))
    return (weights * (direct / member_count - total / (member_count * member_count))).astype(
        jnp.bfloat16
    )


def fourier_tables(lon_count, mode_count):
    positions = jnp.arange(lon_count)
    orders = jnp.arange(mode_count)
    phase = positions[:, None] * orders[None, :] % lon_count
    angle_grid = phase.astype(jnp.float32) * (2.0 * math.pi / lon_count)
    cosine = jnp.cos(angle_grid)
    sine = jnp.sin(angle_grid)
    factor = jnp.where(orders == 0, 1.0, 2.0).astype(jnp.float32)
    synth_table = jnp.concatenate(
        [cosine * factor[None, :], -sine * factor[None, :]], axis=1
    ).astype(jnp.bfloat16)
    analysis_table = jnp.concatenate([cosine.T, -sine.T], axis=0).astype(jnp.bfloat16)
    return (synth_table, analysis_table)


def legendre_table(orders, lat_count, degree_count):
    angles = (jnp.arange(lat_count).astype(jnp.float32) + 0.5) * (math.pi / lat_count)
    cosine = jnp.cos(angles)
    sine = jnp.sin(angles)
    order_f = orders.astype(jnp.float32)[:, None]
    factor_index = jnp.arange(1, lat_count + 1).astype(jnp.float32)
    ratios = jnp.log((2.0 * factor_index - 1.0) / (2.0 * factor_index))
    partial_log = jnp.sum(jnp.where(factor_index[None, :] <= order_f, ratios[None, :], 0.0), axis=1)
    start_log = (
        0.5 * jnp.log(order_f + 0.5) + 0.5 * partial_log[:, None] + order_f * jnp.log(sine)[None, :]
    )
    zeros_start = jnp.zeros((orders.shape[0], lat_count), jnp.float32)

    def advance(state, degree):
        older, newer, log_scale = state
        degree_f = degree.astype(jnp.float32)
        alpha_rec = jnp.sqrt(
            jnp.maximum(4.0 * degree_f * degree_f - 1.0, 1.0)
            / jnp.maximum(degree_f * degree_f - order_f * order_f, 1.0)
        )
        below = degree_f - 1.0
        beta_rec = jnp.sqrt(
            jnp.maximum(below * below - order_f * order_f, 0.0)
            / jnp.maximum(4.0 * below * below - 1.0, 1.0)
        )
        recurred = alpha_rec * (cosine[None, :] * newer - beta_rec * older)
        fresh = jnp.where(degree_f < order_f, 0.0, jnp.where(degree_f == order_f, 1.0, recurred))
        output = fresh * jnp.exp(log_scale)
        norm_value = jnp.where(degree_f < order_f, 1.0, jnp.maximum(jnp.abs(fresh), jnp.abs(newer)))
        return ((newer / norm_value, fresh / norm_value, log_scale + jnp.log(norm_value)), output)

    block_size = math.gcd(degree_count, 32)

    def advance_block(state, block_start):
        rows_out = []
        for offset in range(block_size):
            state, output = advance(state, block_start + offset)
            rows_out.append(output)
        return (state, jnp.stack(rows_out))

    start_state = (zeros_start, zeros_start, start_log)
    block_starts = jnp.arange(degree_count // block_size) * block_size
    final_state, table_blocks = lax.scan(advance_block, start_state, block_starts)
    return table_blocks.reshape(degree_count, orders.shape[0], lat_count)


def shards(
    grid_input, saved_mixed, target, land_weight, mix_weight, degree_gain, up_weight, down_weight
):
    rows_lat = grid_input.shape[1]
    lon_count = grid_input.shape[2]
    channel_count = grid_input.shape[3]
    total_lat = degree_gain.shape[0]
    mode_count = lon_count // 2
    local_modes = mode_count // lax.axis_size("lat")
    flat_saved = saved_mixed.reshape(rows_lat * lon_count, channel_count)
    hidden_pre = jnp.dot(flat_saved, up_weight, preferred_element_type=jnp.float32)
    values, slopes = gelu_parts(hidden_pre)
    activation = values.astype(jnp.bfloat16)
    branch_out = jnp.dot(activation, down_weight, preferred_element_type=jnp.float32)
    member_out = (grid_input.reshape(branch_out.shape).astype(jnp.float32) + branch_out).astype(
        jnp.bfloat16
    )
    member_out = member_out.reshape(rows_lat, lon_count, channel_count)
    lat_start = lax.axis_index("lat") * rows_lat
    local_angles = ((lat_start + jnp.arange(rows_lat)).astype(jnp.float32) + 0.5) * (
        math.pi / total_lat
    )
    weights = (jnp.sin(local_angles)[:, None] * land_weight.astype(jnp.float32))[:, :, None]
    everyone = lax.all_gather(member_out[None], "member", axis=0, tiled=True)
    cotangent = member_term(member_out.astype(jnp.float32), everyone, target, weights)
    act_grad = jnp.dot(
        cotangent.reshape(rows_lat * lon_count, channel_count),
        down_weight.T,
        preferred_element_type=jnp.float32,
    )
    pre_grad = (act_grad * slopes).astype(jnp.bfloat16)
    mixed_grad = jnp.dot(pre_grad, up_weight.T, preferred_element_type=jnp.float32).astype(
        jnp.bfloat16
    )
    mixed_grad = mixed_grad.reshape(rows_lat, lon_count, channel_count)
    synth_table, analysis_table = fourier_tables(lon_count, mode_count)
    wave_grad = jnp.einsum(
        "jnc,nk->jkc", mixed_grad, synth_table, preferred_element_type=jnp.float32
    ).astype(jnp.bfloat16)
    wave_grad = wave_grad.reshape(rows_lat, 2, mode_count, channel_count)
    wave_all = lax.all_to_all(wave_grad, "lat", split_axis=2, concat_axis=0, tiled=True)
    local_orders = lax.axis_index("lat") * local_modes + jnp.arange(local_modes)
    legendre = legendre_table(local_orders, total_lat, total_lat).astype(jnp.bfloat16)
    all_angles = (jnp.arange(total_lat).astype(jnp.float32) + 0.5) * (math.pi / total_lat)
    quad_weight = jnp.sin(all_angles) * (math.pi / total_lat)
    degree_grad = jnp.einsum(
        "lmj,jpmc->lpmc", legendre, wave_all, preferred_element_type=jnp.float32
    )
    gained = (degree_grad * degree_gain[:, None, None, None]).astype(jnp.bfloat16)
    coeff_grad = jnp.einsum(
        "lpmd,cd->lpmc", gained, mix_weight, preferred_element_type=jnp.float32
    ).astype(jnp.bfloat16)
    lat_grad = (
        jnp.einsum("lmj,lpmc->jpmc", legendre, coeff_grad, preferred_element_type=jnp.float32)
        * quad_weight[:, None, None, None]
    )
    lat_grad = lat_grad.astype(jnp.bfloat16)
    returned = lax.all_to_all(lat_grad, "lat", split_axis=0, concat_axis=2, tiled=True)
    spatial = jnp.einsum(
        "jkc,kn->jnc",
        returned.reshape(rows_lat, 2 * mode_count, channel_count),
        analysis_table,
        preferred_element_type=jnp.float32,
    ) * (1.0 / lon_count)
    grad_input = (cotangent.astype(jnp.float32) + spatial).astype(jnp.bfloat16)
    return grad_input[None]


def solution(mesh):
    in_specs = (
        P("member", "lat", None, None),
        P("member", "lat", None, None),
        P("lat", None, None),
        P("lat", None),
        P(),
        P(),
        P(),
        P(),
    )
    out_specs = P("member", "lat", None, None)
    return jax.shard_map(shards, mesh=mesh, in_specs=in_specs, out_specs=out_specs, check_vma=False)
```

profile of v0, /device:TPU:102, one launch (start us, length us, event | category | flops | bytes accessed | tf_op | source)
XLA Modules:
  0.0 666.5 jit_solution(1625304222120287279)
XLA Ops:
  6.5 1.7 copy-done
  8.2 2.5 fusion.73
  10.7 5.0 fusion.18
  16.6 5.7 multiply_convert_fusion.6
  22.3 163.7 %all-gather.2.cloned.1.call-done = bf16[4,6,768,256]{3,2,1,0:T(8,128)(2,1)} async-done(((bf16[1,6,768,256]{3,2,1,0:T(8,128)(2,1)}), bf16[4,6,768,256]{3,2,1,0:T(8,128)(2,1)}) %all-gather.2.cloned.1.call-update) | async-done | bytes 9437200 | tf_op jit(solution)/shard_map/all_gather | solution.py:121
  186.0 9.6 %multiply_convert_fusion.4 = bf16[6,768,256]{2,1,0:T(8,128)(2,1)} fusion(bf16[6,768,256]{2,1,0:T(8,128)(2,1)} %bitcast.687, bf16[6,768,256]{2,1,0:T(8,128)(2,1)} %param.12, bf16[4,6,768,256]{3,2,1,0:T(8,128)(2,1)} %all-gather.2.cloned.1.call-done, f32[6,768]{1,0:T(8,128)S(1)} %convert_multiply_fusion.1), kind=kLoop, calls=%fused_computation.291 | loop fusion | flops 40108032 | bytes 16533504 | tf_op jit(solution)/shard_map/convert_element_type | solution.py:32
  195.7 10.4 %convolution_convert_fusion = bf16[4608,256]{1,0:T(8,128)(2,1)} fusion(bf16[256,512]{1,0:T(8,128)(2,1)S(1)} %copy-done.2, f32[4608,512]{1,0:T(8,128)} %copy-done.1, bf16[4608,256]{1,0:T(8,128)(2,1)} %bitcast.688, bf16[512,256]{1,0:T(8,128)(2,1)} %param.17), kind=kOutput, calls=%fused_computation.286 | convolution fusion | flops 2461925376 | bytes 14680064 | tf_op jit(solution)/shard_map/dot_general | solution.py:129
  206.0 3.9 convolution_convert_fusion.1
  209.9 3.8 copy.16
  213.8 13.1 %all-to-all-start = ((bf16[6,2,384,256]{3,1,0,2:T(2,128)(2,1)}), bf16[6,2,384,256]{3,1,0,2:T(2,128)(2,1)}, u32[]{:S(2)}, u32[]{:S(2)}) async-start(bf16[6,2,384,256]{3,1,0,2:T(2,128)(2,1)} %copy.16), calls=%async_computation | async-start | bytes 4718592 | tf_op jit(solution)/shard_map/all_to_all | solution.py:138
  226.9 324.8 %while.23 = (s32[]{:T(128)}, f32[6,384]{1,0:T(8,128)S(1)}, f32[6,384]{1,0:T(8,128)S(1)}, f32[6,384]{1,0:T(8,128)S(1)}, bf16[12,32,6,384]{3,2,1,0:T(8,128)(2,1)},...) while((s32[]{:T(128)}, f32[6,384]{1,0:T(8,128)S(1)}, ...), condition=%wide.region_2.3_spmd.clone.clone.clone.clone, body=%wide.region_1.2_spmd.clone.clone.clone.clone.sunk | while | flops 1467105 | bytes 3442120 | solution.py:94
  388.6 0.7 bitcast_dynamic-update-slice_fusion.2
  523.9 0.7 bitcast_dynamic-update-slice_fusion.2
  551.0 0.7 bitcast_dynamic-update-slice_fusion.2
  551.8 4.7 copy.18
  556.6 6.3 fusion.25
  562.9 5.5 fusion.27
  568.4 6.9 %copy.24 = bf16[384,2,6,256]{3,1,2,0:T(2,128)(2,1)} copy(bf16[384,2,6,256]{0,3,1,2:T(8,128)(2,1)} %fusion.27) | data formatting | bytes 4718592 | tf_op jit(solution)/shard_map/convert_element_type | solution.py:154
  575.2 13.0 %all-to-all-start.1 = ((bf16[384,2,6,256]{3,1,2,0:T(2,128)(2,1)}), bf16[384,2,6,256]{3,1,2,0:T(2,128)(2,1)}, u32[]{:S(2)}, u32[]{:S(2)}) async-start(bf16[384,2,6,256]{3,1,2,0:T(2,128)(2,1)} %copy.24), calls=%async_computation.1 | async-start | bytes 4718592 | tf_op jit(solution)/shard_map/all_to_all | solution.py:155
  588.2 5.0 negate_convert_fusion
  593.3 51.5 %all-to-all-done.1 = bf16[384,2,6,256]{3,1,2,0:T(2,128)(2,1)} async-done(((bf16[384,2,6,256]{3,1,2,0:T(2,128)(2,1)}), bf16[384,2,6,256]{3,1,2,0:T(2,128)(2,1)}, u32[]{:S(2)}, u32[]{:S(2)}) %all-to-all-start.1) | async-done | bytes 2359328 | tf_op jit(solution)/shard_map/all_to_all | solution.py:155
  644.8 3.9 copy.25
  648.7 5.2 reshape.1991
  653.8 5.8 fusion.28
  (1230 shorter events, 65.2 us)
Async XLA Ops:
  6.5 1.7 copy-start
  6.5 179.5 %all-gather.2.cloned.1.call-start = ((), (), s32[]{:S(2)}) async-start(), calls=%async_computation.2 | async-start | bytes 11796480 | tf_op jit(solution)/shard_map/all_gather | solution.py:121
  8.2 2.5 copy-start.4
  8.2 2.5 copy-start.5
  10.7 5.1 copy-start.1
  15.8 0.7 copy-start.3
  186.0 9.6 %copy-start.2 = (bf16[256,512]{1,0:T(8,128)(2,1)S(1)}, bf16[256,512]{1,0:T(8,128)(2,1)}, u32[]{:S(2)}) copy-start(bf16[256,512]{1,0:T(8,128)(2,1)} %param.16) | copy-start | bytes 786436
  213.8 338.0 %all-to-all-start = ((bf16[6,2,384,256]{3,1,0,2:T(2,128)(2,1)}), bf16[6,2,384,256]{3,1,0,2:T(2,128)(2,1)}, u32[]{:S(2)}, u32[]{:S(2)}) async-start(bf16[6,2,384,256]{3,1,0,2:T(2,128)(2,1)} %copy.16), calls=%async_computation | async-start | bytes 4718592 | tf_op jit(solution)/shard_map/all_to_all | solution.py:138
  551.8 4.8 copy-start.6
  551.8 4.8 copy-start.7
  575.2 69.6 %all-to-all-start.1 = ((bf16[384,2,6,256]{3,1,2,0:T(2,128)(2,1)}), bf16[384,2,6,256]{3,1,2,0:T(2,128)(2,1)}, u32[]{:S(2)}, u32[]{:S(2)}) async-start(bf16[384,2,6,256]{3,1,2,0:T(2,128)(2,1)} %copy.24), calls=%async_computation.1 | async-start | bytes 4718592 | tf_op jit(solution)/shard_map/all_to_all | solution.py:155
Sparse Core Ops, SparseCore 0:
  15.9 170.0 all-gather.1
where the time goes:
time: 672 us; the launch traced here: 667 us
  loops' own time  258 us (38%)
  waiting for transfers between devices  215 us (32%)
  other arithmetic  71.7 us (11%)
  local copies, waits for them, and re-layouts  42.2 us (6%)
  matrix products  39.4 us (6%)
  starting transfers between devices  26.1 us (4%)
  between operations  13.6 us (2%)
    another operation x1, loops' own time, legendre_table(): lax.scan(advance_block, start_state, block_starts)  258 us
    all_gather x1, waiting for transfers between devices, shards(): everyone = lax.all_gather(member_out[None], 'member', axis=0, tiled=True)  164 us
    all_to_all x1, waiting for transfers between devices, shards(): lax.all_to_all(lat_grad, 'lat', split_axis=0, concat_axis=2, tiled=True)  51.5 us
    while x372, other arithmetic  38.2 us
  transfers between devices with their start and end apart: 3, of which 2 were waited for; matrix products, arithmetic and copies ran while one was open for 12% of the time, Pallas kernels for 0%

commit v1 on v0

--- a/solution.py
+++ b/solution.py
@@ -1,8 +1,11 @@
+import functools
 import math
 
 import jax
 import jax.numpy as jnp
 from jax import lax
+from jax.experimental import pallas as pl
+from jax.experimental.pallas import tpu as pltpu
 from jax.sharding import PartitionSpec as P
 
 kappa_gelu = 0.7978845608
@@ -23,15 +26,22 @@
     return difference * lax.rsqrt(difference * difference + smooth_square)
 
 
-def member_term(own_values, everyone, target, weights):
+def member_terms(everyone, target, weights):
     member_count = everyone.shape[0]
-    total = jnp.zeros(own_values.shape, jnp.float32)
-    for slot in range(member_count):
-        total = total + slope_abs(own_values - everyone[slot].astype(jnp.float32))
-    direct = slope_abs(own_values - target.astype(jnp.float32))
-    return (weights * (direct / member_count - total / (member_count * member_count))).astype(
-        jnp.bfloat16
-    )
+    values = [everyone[slot].astype(jnp.float32) for slot in range(member_count)]
+    totals = [jnp.zeros(target.shape, jnp.float32) for slot in range(member_count)]
+    for first in range(member_count):
+        for second in range(first + 1, member_count):
+            slope = slope_abs(values[first] - values[second])
+            totals[first] = totals[first] + slope
+            totals[second] = totals[second] - slope
+    wanted = target.astype(jnp.float32)
+    terms = [
+        weights
+        * (slope_abs(values[slot] - wanted) / member_count - totals[slot] / (member_count * member_count))
+        for slot in range(member_count)
+    ]
+    return jnp.stack(terms).astype(jnp.bfloat16)
 
 
 def fourier_tables(lon_count, mode_count):
@@ -49,50 +59,63 @@
     return (synth_table, analysis_table)
 
 
-def legendre_table(orders, lat_count, degree_count):
-    angles = (jnp.arange(lat_count).astype(jnp.float32) + 0.5) * (math.pi / lat_count)
+def legendre_kernel(block, start_ref, order_ref, cosine_ref, table_ref, rows_ref):
+    degree_count = rows_ref.shape[0]
+    order_count = table_ref.shape[0]
+    order_f = order_ref[...]
+    cosine = cosine_ref[...]
+    zeros = jnp.zeros(cosine.shape, jnp.float32)
+
+    def advance_block(step, state):
+        older, newer, log_scale = state
+        half_scale = jnp.exp(0.5 * log_scale)
+        for offset in range(block):
+            degree = step * block + offset
+            degree_f = degree.astype(jnp.float32)
+            below = degree_f - 1.0
+            alpha_rec = jnp.sqrt(
+                jnp.maximum(4.0 * degree_f * degree_f - 1.0, 1.0)
+                / jnp.maximum(degree_f * degree_f - order_f * order_f, 1.0)
+            )
+            beta_rec = jnp.sqrt(
+                jnp.maximum(below * below - order_f * order_f, 0.0)
+                / jnp.maximum(4.0 * below * below - 1.0, 1.0)
+            )
+            recurred = alpha_rec * (cosine * newer - beta_rec * older)
+            fresh = jnp.where(
+                degree_f < order_f, 0.0, jnp.where(degree_f == order_f, 1.0, recurred)
+            )
+            rows_ref[degree] = (fresh * half_scale) * half_scale
+            older, newer = newer, fresh
+        largest = jnp.maximum(jnp.abs(older), jnp.abs(newer))
+        norm_value = jnp.where(largest > 0.0, largest, 1.0)
+        return (older / norm_value, newer / norm_value, log_scale + jnp.log(norm_value))
+
+    lax.fori_loop(0, degree_count // block, advance_block, (zeros, zeros, start_ref[...]))
+    for slot in range(order_count):
+        table_ref[slot] = rows_ref[:, slot, :].astype(jnp.bfloat16)
+
+
+def legendre_table(orders, angles, degree_count):
     cosine = jnp.cos(angles)
     sine = jnp.sin(angles)
+    order_count = orders.shape[0]
+    padded = (order_count + 7) // 8 * 8
+    orders = jnp.concatenate([orders, jnp.broadcast_to(orders[:1], (padded - order_count,))])
     order_f = orders.astype(jnp.float32)[:, None]
-    factor_index = jnp.arange(1, lat_count + 1).astype(jnp.float32)
+    factor_index = jnp.arange(1, degree_count + 1).astype(jnp.float32)
     ratios = jnp.log((2.0 * factor_index - 1.0) / (2.0 * factor_index))
     partial_log = jnp.sum(jnp.where(factor_index[None, :] <= order_f, ratios[None, :], 0.0), axis=1)
     start_log = (
         0.5 * jnp.log(order_f + 0.5) + 0.5 * partial_log[:, None] + order_f * jnp.log(sine)[None, :]
     )
-    zeros_start = jnp.zeros((orders.shape[0], lat_count), jnp.float32)
-
-    def advance(state, degree):
-        older, newer, log_scale = state
-        degree_f = degree.astype(jnp.float32)
-        alpha_rec = jnp.sqrt(
-            jnp.maximum(4.0 * degree_f * degree_f - 1.0, 1.0)
-            / jnp.maximum(degree_f * degree_f - order_f * order_f, 1.0)
-        )
-        below = degree_f - 1.0
-        beta_rec = jnp.sqrt(
-            jnp.maximum(below * below - order_f * order_f, 0.0)
-            / jnp.maximum(4.0 * below * below - 1.0, 1.0)
-        )
-        recurred = alpha_rec * (cosine[None, :] * newer - beta_rec * older)
-        fresh = jnp.where(degree_f < order_f, 0.0, jnp.where(degree_f == order_f, 1.0, recurred))
-        output = fresh * jnp.exp(log_scale)
-        norm_value = jnp.where(degree_f < order_f, 1.0, jnp.maximum(jnp.abs(fresh), jnp.abs(newer)))
-        return ((newer / norm_value, fresh / norm_value, log_scale + jnp.log(norm_value)), output)
-
-    block_size = math.gcd(degree_count, 32)
-
-    def advance_block(state, block_start):
-        rows_out = []
-        for offset in range(block_size):
-            state, output = advance(state, block_start + offset)
-            rows_out.append(output)
-        return (state, jnp.stack(rows_out))
-
-    start_state = (zeros_start, zeros_start, start_log)
-    block_starts = jnp.arange(degree_count // block_size) * block_size
-    final_state, table_blocks = lax.scan(advance_block, start_state, block_starts)
-    return table_blocks.reshape(degree_count, orders.shape[0], lat_count)
+    shape = start_log.shape
+    return pl.pallas_call(
+        functools.partial(legendre_kernel, 16),
+        out_shape=jax.ShapeDtypeStruct((order_count, degree_count, shape[1]), jnp.bfloat16),
+        scratch_shapes=[pltpu.VMEM((degree_count,) + shape, jnp.float32)],
+        compiler_params=pltpu.CompilerParams(vmem_limit_bytes=32 * 2**20),
+    )(start_log, jnp.broadcast_to(order_f, shape), jnp.broadcast_to(cosine[None, :], shape))
 
 
 def shards(
@@ -118,8 +141,17 @@
         math.pi / total_lat
     )
     weights = (jnp.sin(local_angles)[:, None] * land_weight.astype(jnp.float32))[:, :, None]
-    everyone = lax.all_gather(member_out[None], "member", axis=0, tiled=True)
-    cotangent = member_term(member_out.astype(jnp.float32), everyone, target, weights)
+    member_count = lax.axis_size("member")
+    part = lon_count // member_count
+    part_start = lax.axis_index("member") * part
+    everyone = lax.all_to_all(
+        member_out.reshape(rows_lat, member_count, part, channel_count), "member", 1, 0
+    )
+    own_target = lax.dynamic_slice_in_dim(target, part_start, part, 1)
+    own_weights = lax.dynamic_slice_in_dim(weights, part_start, part, 1)
+    cotangent = member_terms(everyone, own_target, own_weights)
+    cotangent = lax.all_to_all(cotangent, "member", 0, 1)
+    cotangent = cotangent.reshape(rows_lat, lon_count, channel_count)
     act_grad = jnp.dot(
         cotangent.reshape(rows_lat * lon_count, channel_count),
         down_weight.T,
@@ -137,18 +169,18 @@
     wave_grad = wave_grad.reshape(rows_lat, 2, mode_count, channel_count)
     wave_all = lax.all_to_all(wave_grad, "lat", split_axis=2, concat_axis=0, tiled=True)
     local_orders = lax.axis_index("lat") * local_modes + jnp.arange(local_modes)
-    legendre = legendre_table(local_orders, total_lat, total_lat).astype(jnp.bfloat16)
     all_angles = (jnp.arange(total_lat).astype(jnp.float32) + 0.5) * (math.pi / total_lat)
+    legendre = legendre_table(local_orders, all_angles, total_lat)
     quad_weight = jnp.sin(all_angles) * (math.pi / total_lat)
     degree_grad = jnp.einsum(
-        "lmj,jpmc->lpmc", legendre, wave_all, preferred_element_type=jnp.float32
+        "mlj,jpmc->lpmc", legendre, wave_all, preferred_element_type=jnp.float32
     )
     gained = (degree_grad * degree_gain[:, None, None, None]).astype(jnp.bfloat16)
     coeff_grad = jnp.einsum(
         "lpmd,cd->lpmc", gained, mix_weight, preferred_element_type=jnp.float32
     ).astype(jnp.bfloat16)
     lat_grad = (
-        jnp.einsum("lmj,lpmc->jpmc", legendre, coeff_grad, preferred_element_type=jnp.float32)
+        jnp.einsum("mlj,lpmc->jpmc", legendre, coeff_grad, preferred_element_type=jnp.float32)
         * quad_weight[:, None, None, None]
     )
     lat_grad = lat_grad.astype(jnp.bfloat16)

time: 672 us -> 322 us (0.48)
  loops' own time: 258 us -> 0 us
  other arithmetic: 71.7 us -> 17.9 us
  waiting for transfers between devices: 215 us -> 187 us
  between operations: 13.6 us -> 0.17 us
  local copies, waits for them, and re-layouts: 42.2 us -> 32.3 us
  starting transfers between devices: 26.1 us -> 35.5 us
  Pallas kernels: 0 us -> 8.92 us
    another operation x1 -> x0, loops' own time: 258 us -> none  [legendre_table(): lax.scan(advance_block, start_state, block_starts)]
    all_gather x1 -> x0, waiting for transfers between devices: 164 us -> none  [shards(): everyone = lax.all_gather(member_out[None], 'member', axis=0, tiled=True)]
    all_to_all x0 -> x2, waiting for transfers between devices: none -> 96.7 us  [the longest x1 50.7 us: shards(): lax.all_to_all(member_out.reshape(rows_lat, member_count, part, channel_c...]
    all_to_all x1, waiting for transfers between devices: 0.01 us -> 45.7 us  [shards(): lax.all_to_all(wave_grad, 'lat', split_axis=2, concat_axis=0, tiled=True)]
    while x372 -> x0, other arithmetic: 38.2 us -> none
    all_to_all x0 -> x2, starting transfers between devices: none -> 11.9 us  [the longest x1 6.82 us: shards(): cotangent = lax.all_to_all(cotangent, 'member', 0, 1)]
    convert_element_type x3 -> x2, other arithmetic: 9.63 us -> 0.04 us  [the longest x1 0.04 us: legendre_table(): order_f = orders.astype(jnp.float32)[:, None]]
    pallas_call x0 -> x1, Pallas kernels: none -> 8.92 us  [legendre_table(): pl.pallas_call(functools.partial(legendre_kernel, 16), out_shape=jax.Shap...]
  transfers between devices with their start and end apart: 3 -> 4, of which waited for: 2 -> 4; matrix products, arithmetic and copies ran while one was open for 12% -> 4% of each run, Pallas kernels for 0% -> 3%
where the time goes in v1:
time: 322 us; the launch traced here: 319 us
  waiting for transfers between devices  187 us (58%)
  matrix products  37.4 us (12%)
  starting transfers between devices  35.5 us (11%)
  local copies, waits for them, and re-layouts  32.3 us (10%)
  other arithmetic  17.9 us (6%)
  Pallas kernels  8.92 us (3%)
    all_to_all x1, waiting for transfers between devices, shards(): lax.all_to_all(member_out.reshape(rows_lat, member_count, part, channel_c...  50.7 us
    all_to_all x1, waiting for transfers between devices, shards(): cotangent = lax.all_to_all(cotangent, 'member', 0, 1)  46 us
    all_to_all x1, waiting for transfers between devices, shards(): lax.all_to_all(wave_grad, 'lat', split_axis=2, concat_axis=0, tiled=True)  45.7 us
    all_to_all x1, waiting for transfers between devices, shards(): lax.all_to_all(lat_grad, 'lat', split_axis=0, concat_axis=2, tiled=True)  44.4 us
    all_to_all x1, starting transfers between devices, shards(): lax.all_to_all(wave_grad, 'lat', split_axis=2, concat_axis=0, tiled=True)  13.7 us
    dot_general x1, matrix products, shards(): jnp.dot(pre_grad, up_weight.T, preferred_element_type=jnp.float32)  10.4 us
    another operation x2, other arithmetic  10.1 us
    all_to_all x1, starting transfers between devices, shards(): lax.all_to_all(lat_grad, 'lat', split_axis=0, concat_axis=2, tiled=True)  9.91 us
  transfers between devices with their start and end apart: 4, of which 4 were waited for; matrix products, arithmetic and copies ran while one was open for 4% of the time, Pallas kernels for 3%

profile of v1, /device:TPU:102, one launch (start us, length us, event | category | flops | bytes accessed | tf_op | source)
XLA Modules:
  0.0 318.9 jit_solution(14902578104626058754)
XLA Ops:
  4.2 3.8 %fusion.7 = bf16[4608,256]{1,0:T(8,128)(2,1)S(1)} fusion(bf16[512,256]{1,0:T(8,128)(2,1)S(1)} %copy-done.4, f32[4608,512]{1,0:T(8,128)S(1)} %fusion.69, bf16[4608,256]{1,0:T(8,128)(2,1)S(1)} %bitcast.129), kind=kOutput, calls=%fused_computation.11 | convolution fusion | flops 1232732160 | bytes 14417920 | tf_op jit(solution)/shard_map/dot_general | solution.py:134
  9.6 5.1 %all-to-all-start = ((bf16[1,6,4,192,256]{4,3,1,0,2:T(8,128)(2,1)}), bf16[1,6,4,192,256]{4,3,1,0,2:T(8,128)(2,1)}, u32[]{:S(2)}, u32[]{:S(2)}) async-start(bf16[1,6,4,192,256]{4,3,1,0,2:T(8,128)(2,1)} %copy.20), calls=%async_computation | async-start | bytes 4718592 | tf_op jit(solution)/shard_map/all_to_all | solution.py:147
  15.5 50.7 %all-to-all-done = bf16[1,6,4,192,256]{4,3,1,0,2:T(8,128)(2,1)} async-done(((bf16[1,6,4,192,256]{4,3,1,0,2:T(8,128)(2,1)}), bf16[1,6,4,192,256]{4,3,1,0,2:T(8,128)(2,1)}, u32[]{:S(2)}, u32[]{:S(2)}) %all-to-all-start) | async-done | bytes 2359328 | tf_op jit(solution)/shard_map/all_to_all | solution.py:147
  66.2 4.8 %fusion.46 = (bf16[1,6,1,192,256]{4,3,1,2,0:T(8,128)(2,1)S(1)}, bf16[1,6,1,192,256]{4,3,1,2,0:T(8,128)(2,1)S(1)}, bf16[1,6,1,192,256]{4,3,1,2,0:T(8,128)(2,1)S(1)}, bf16[1,6,1,192,256]{4,3,1,2,0:T(8,128)(2,1)S(1)}) fusion(f32[6,192]{1,0:T(8,128)S(1)} %fusion.51, bf16[4,1,6,1,192,256]{5,4,2,3,1,0:T(8,128)(2,1)} %bitcast.5, ...), kind=kLoop, calls=%fused_computation.82 | loop fusion | flops 22413312 | bytes 5313028 | tf_op jit(solution)/shard_map/stack | solution.py:44
  72.7 6.8 %all-to-all-start.1 = ((bf16[4,6,1,192,256]{4,3,1,2,0:T(8,128)(2,1)}), bf16[4,6,1,192,256]{4,3,1,2,0:T(8,128)(2,1)}, u32[]{:S(2)}, u32[]{:S(2)}) async-start(bf16[4,6,1,192,256]{4,3,1,2,0:T(8,128)(2,1)} %pad_maximum_fusion), calls=%async_computation.1 | async-start | bytes 4718592 | tf_op jit(solution)/shard_map/all_to_all | solution.py:153
  79.5 5.1 %multiply_convert_fusion.5 = (bf16[768,384]{0,1:T(8,128)(2,1)S(1)}, bf16[768,384]{0,1:T(8,128)(2,1)S(1)}) fusion(f32[384]{0:T(512)S(1)} %fusion.57), kind=kLoop, calls=%fused_computation.57 | loop fusion | flops 4128768 | bytes 1181184 | tf_op jit(solution)/shard_map/convert.6
  84.6 46.0 %all-to-all-done.1 = bf16[4,6,1,192,256]{4,3,1,2,0:T(8,128)(2,1)} async-done(((bf16[4,6,1,192,256]{4,3,1,2,0:T(8,128)(2,1)}), bf16[4,6,1,192,256]{4,3,1,2,0:T(8,128)(2,1)}, u32[]{:S(2)}, u32[]{:S(2)}) %all-to-all-start.1) | async-done | bytes 2359328 | tf_op jit(solution)/shard_map/all_to_all | solution.py:153
  130.6 3.3 %copy.24 = bf16[4,6,1,192,256]{4,3,0,1,2:T(8,128)(2,1)} copy(bf16[4,6,1,192,256]{4,3,1,2,0:T(8,128)(2,1)} %all-to-all-done.1) | data formatting | bytes 4718592 | tf_op jit(solution)/shard_map/all_to_all | solution.py:153
  133.9 10.4 %convolution_convert_fusion = bf16[4608,256]{1,0:T(8,128)(2,1)} fusion(bf16[256,512]{1,0:T(8,128)(2,1)} %param.14, f32[4608,512]{1,0:T(8,128)} %copy-done.2, bf16[4608,256]{1,0:T(8,128)(2,1)} %bitcast.122, bf16[512,256]{1,0:T(8,128)(2,1)} %param.15), kind=kOutput, calls=%fused_computation.12 | convolution fusion | flops 2461925376 | bytes 14680064 | tf_op jit(solution)/shard_map/dot_general | solution.py:161
  144.2 3.7 %convolution_convert_fusion.1 = bf16[768,6,256]{2,0,1:T(8,128)(2,1)S(1)} fusion(bf16[6,768,256]{2,1,0:T(8,128)(2,1)} %bitcast.130, bf16[768,384]{0,1:T(8,128)(2,1)S(1)} %get-tuple-element.10, bf16[768,384]{0,1:T(8,128)(2,1)S(1)} %get-tuple-element.9), kind=kOutput, calls=%fused_computation.41 | convolution fusion | flops 1815478272 | bytes 5898240 | tf_op jit(solution)/shard_map/jnc,nk->jkc/dot_general | solution.py:166
  147.9 3.8 %copy.25 = bf16[6,2,384,256]{3,1,0,2:T(2,128)(2,1)} copy(bf16[6,2,384,256]{3,2,1,0:T(8,128)(2,1)S(1)} %bitcast.124) | data formatting | bytes 4718592 | tf_op jit(solution)/shard_map/reshape | solution.py:169
  151.7 13.7 %all-to-all-start.2 = ((bf16[6,2,384,256]{3,1,0,2:T(2,128)(2,1)}), bf16[6,2,384,256]{3,1,0,2:T(2,128)(2,1)}, u32[]{:S(2)}, u32[]{:S(2)}) async-start(bf16[6,2,384,256]{3,1,0,2:T(2,128)(2,1)} %copy.25), calls=%async_computation.2 | async-start | bytes 4718592 | tf_op jit(solution)/shard_map/all_to_all | solution.py:170
  166.0 8.9 %shard_map.82 = bf16[6,384,384]{2,1,0:T(8,128)(2,1)S(1)} custom-call(f32[8,384]{1,0:T(8,128)S(1)} %multiply_add_fusion.1.start_ref, f32[8,384]{1,0:T(8,128)S(1)} %le.14.order_ref, f32[8,384]{1,0:T(8,128)S(1)} %broadcast_in_dim.31.cosine_ref), custom_call_target="tpu_custom_call" | custom-call | tf_op jit(solution)/shard_map/pallas_call | solution.py:113
  176.2 45.7 %all-to-all-done.2 = bf16[6,2,384,256]{3,1,0,2:T(2,128)(2,1)} async-done(((bf16[6,2,384,256]{3,1,0,2:T(2,128)(2,1)}), bf16[6,2,384,256]{3,1,0,2:T(2,128)(2,1)}, u32[]{:S(2)}, u32[]{:S(2)}) %all-to-all-start.2) | async-done | bytes 2359328 | tf_op jit(solution)/shard_map/all_to_all | solution.py:170
  221.9 4.7 %copy.27 = bf16[64,6,2,6,256]{4,2,3,1,0:T(2,128)(2,1)} copy(bf16[64,6,2,6,256]{4,2,1,3,0:T(2,128)(2,1)} %bitcast.33) | data formatting | bytes 4718592 | tf_op jit(solution)/shard_map/all_to_all | solution.py:170
  226.6 6.1 %fusion.14 = bf16[384,2,6,256]{3,0,1,2:T(8,128)(2,1)} fusion(f32[384]{0:T(512)S(1)} %copy-done.6, bf16[384,2,6,256]{3,1,2,0:T(2,128)(2,1)} %bitcast.125, bf16[6,384,384]{2,1,0:T(8,128)(2,1)} %copy-done.1, bf16[256,256]{1,0:T(8,128)(2,1)S(1)} %copy-done.5), kind=kOutput, calls=%fused_computation.22 | convolution fusion | flops 1512308736 | bytes 6620672 | tf_op jit(solution)/shard_map/lpmd,cd->lpmc/dot_general | solution.py:179
  232.7 5.3 %fusion.16 = bf16[384,2,6,256]{0,3,1,2:T(8,128)(2,1)} fusion(f32[384]{0:T(512)S(1)} %fusion.55, bf16[384,2,6,256]{3,0,1,2:T(8,128)(2,1)} %fusion.14, bf16[6,384,384]{2,1,0:T(8,128)(2,1)} %copy-done.1), kind=kOutput, calls=%fused_computation.23 | convolution fusion | flops 908328960 | bytes 6489600 | tf_op jit(solution)/shard_map/mlj,lpmc->jpmc/dot_general | solution.py:183
  238.0 6.8 %copy.31 = bf16[384,2,6,256]{3,1,2,0:T(2,128)(2,1)} copy(bf16[384,2,6,256]{0,3,1,2:T(8,128)(2,1)} %fusion.16) | data formatting | bytes 4718592 | tf_op jit(solution)/shard_map/convert_element_type | solution.py:186
  244.8 9.9 %all-to-all-start.3 = ((bf16[384,2,6,256]{3,1,2,0:T(2,128)(2,1)}), bf16[384,2,6,256]{3,1,2,0:T(2,128)(2,1)}, u32[]{:S(2)}, u32[]{:S(2)}) async-start(bf16[384,2,6,256]{3,1,2,0:T(2,128)(2,1)} %copy.31), calls=%async_computation.3 | async-start | bytes 4718592 | tf_op jit(solution)/shard_map/all_to_all | solution.py:187
  254.7 5.0 %negate_convert_fusion = (bf16[384,768]{0,1:T(8,128)(2,1)S(1)}, bf16[384,768]{0,1:T(8,128)(2,1)S(1)}) fusion(), kind=kLoop, calls=%fused_computation.61 | loop fusion | flops 3538944 | bytes 1179648 | tf_op jit(solution)/shard_map/convert.9
  259.7 44.4 %all-to-all-done.3 = bf16[384,2,6,256]{3,1,2,0:T(2,128)(2,1)} async-done(((bf16[384,2,6,256]{3,1,2,0:T(2,128)(2,1)}), bf16[384,2,6,256]{3,1,2,0:T(2,128)(2,1)}, u32[]{:S(2)}, u32[]{:S(2)}) %all-to-all-start.3) | async-done | bytes 2359328 | tf_op jit(solution)/shard_map/all_to_all | solution.py:187
  304.1 3.9 %copy.32 = bf16[6,2,64,6,256]{4,3,2,1,0:T(8,128)(2,1)} copy(bf16[6,2,64,6,256]{4,1,3,0,2:T(2,128)(2,1)} %bitcast.42) | data formatting | bytes 4718592 | tf_op jit(solution)/shard_map/all_to_all | solution.py:187
  308.0 5.2 %reshape.155 = bf16[6,768,256]{2,1,0:T(8,128)(2,1)} reshape(bf16[6,2,64,6,256]{4,3,2,1,0:T(8,128)(2,1)} %copy.32) | data formatting | bytes 4718592 | tf_op jit(solution)/shard_map/reshape | solution.py:190
  313.2 5.8 %fusion.17 = bf16[1,6,768,256]{3,2,1,0:T(8,128)(2,1)} fusion(bf16[6,768,256]{2,1,0:T(8,128)(2,1)} %bitcast.123, bf16[6,768,256]{2,1,0:T(8,128)(2,1)} %reshape.155, bf16[384,768]{0,1:T(8,128)(2,1)S(1)} %get-tuple-element.11, bf16[384,768]{0,1:T(8,128)(2,1)S(1)} %get-tuple-element.12), kind=kOutput, calls=%fused_computation.24 | convolution fusion | flops 1819017216 | bytes 8257536 | tf_op jit(solution)/shard_map/jkc,kn->jnc/dot_general | solution.py:188
  (32 shorter events, 10.1 us)
Async XLA Ops:
  0.0 1.7 copy-start
  1.7 2.5 copy-start.3
  1.7 2.5 copy-start.4
  4.2 3.8 %copy-start.2 = (f32[4608,512]{1,0:T(8,128)}, f32[4608,512]{1,0:T(8,128)S(1)}, u32[]{:S(2)}) copy-start(f32[4608,512]{1,0:T(8,128)S(1)} %fusion.69) | copy-start | bytes 28311556
  9.6 56.6 %all-to-all-start = ((bf16[1,6,4,192,256]{4,3,1,0,2:T(8,128)(2,1)}), bf16[1,6,4,192,256]{4,3,1,0,2:T(8,128)(2,1)}, u32[]{:S(2)}, u32[]{:S(2)}) async-start(bf16[1,6,4,192,256]{4,3,1,0,2:T(8,128)(2,1)} %copy.20), calls=%async_computation | async-start | bytes 4718592 | tf_op jit(solution)/shard_map/all_to_all | solution.py:147
  72.7 57.9 %all-to-all-start.1 = ((bf16[4,6,1,192,256]{4,3,1,2,0:T(8,128)(2,1)}), bf16[4,6,1,192,256]{4,3,1,2,0:T(8,128)(2,1)}, u32[]{:S(2)}, u32[]{:S(2)}) async-start(bf16[4,6,1,192,256]{4,3,1,2,0:T(8,128)(2,1)} %pad_maximum_fusion), calls=%async_computation.1 | async-start | bytes 4718592 | tf_op jit(solution)/shard_map/all_to_all | solution.py:153
  151.7 70.1 %all-to-all-start.2 = ((bf16[6,2,384,256]{3,1,0,2:T(2,128)(2,1)}), bf16[6,2,384,256]{3,1,0,2:T(2,128)(2,1)}, u32[]{:S(2)}, u32[]{:S(2)}) async-start(bf16[6,2,384,256]{3,1,0,2:T(2,128)(2,1)} %copy.25), calls=%async_computation.2 | async-start | bytes 4718592 | tf_op jit(solution)/shard_map/all_to_all | solution.py:170
  174.9 1.3 copy-start.1
  221.9 4.7 %copy-start.5 = (bf16[256,256]{1,0:T(8,128)(2,1)S(1)}, bf16[256,256]{1,0:T(8,128)(2,1)}, u32[]{:S(2)}) copy-start(bf16[256,256]{1,0:T(8,128)(2,1)} %param.12) | copy-start | bytes 393220
  221.9 4.7 %copy-start.6 = (f32[384]{0:T(512)S(1)}, f32[384]{0:T(512)}, u32[]{:S(2)}) copy-start(f32[384]{0:T(512)} %param.13) | copy-start | bytes 4612
  244.8 59.4 %all-to-all-start.3 = ((bf16[384,2,6,256]{3,1,2,0:T(2,128)(2,1)}), bf16[384,2,6,256]{3,1,2,0:T(2,128)(2,1)}, u32[]{:S(2)}, u32[]{:S(2)}) async-start(bf16[384,2,6,256]{3,1,2,0:T(2,128)(2,1)} %copy.31), calls=%async_computation.3 | async-start | bytes 4718592 | tf_op jit(solution)/shard_map/all_to_all | solution.py:187

commit v2 on v1

v2 whole, which is shorter than its diff:
```python
import functools
import math

import jax
import jax.numpy as jnp
import ml_dtypes
import numpy as np
from jax import lax
from jax.experimental import pallas as pl
from jax.experimental.pallas import tpu as pltpu
from jax.sharding import PartitionSpec as P

kappa_gelu = 0.7978845608
cubic_gelu = 0.044715
smooth_square = 0.25
pair_rows = 2
MESH = pl.DeviceIdType.MESH


def gelu_parts(inputs):
    squared = inputs * inputs
    tanh_part = jnp.tanh(kappa_gelu * inputs * (1.0 + cubic_gelu * squared))
    half_sum = 0.5 * (1.0 + tanh_part)
    values = inputs * half_sum
    slopes = half_sum + 0.5 * inputs * (1.0 - tanh_part * tanh_part) * (
        kappa_gelu + (3.0 * cubic_gelu * kappa_gelu) * squared
    )
    return (values, slopes)


def slope_abs(difference):
    return difference * lax.rsqrt(difference * difference + smooth_square)


def dot_nn(lhs, rhs):
    return lax.dot_general(lhs, rhs, (((1,), (0,)), ((), ())), preferred_element_type=jnp.float32)


def dot_nt(lhs, rhs):
    return lax.dot_general(lhs, rhs, (((1,), (1,)), ((), ())), preferred_element_type=jnp.float32)


def dot_tn(lhs, rhs):
    return lax.dot_general(lhs, rhs, (((0,), (0,)), ((), ())), preferred_element_type=jnp.float32)


def fourier_tables(lon_count, plane_count, orders_each):
    mode_count = lon_count // 2
    orders = np.arange(mode_count).reshape(2, plane_count, orders_each)
    positions = np.arange(lon_count)
    phase = (orders[..., None] * positions) % lon_count
    angles = phase.astype(np.float32) * np.float32(2.0 * math.pi / lon_count)
    cosine = np.cos(angles)
    sine = np.sin(angles)
    factor = np.where(orders == 0, 1.0, 2.0).astype(np.float32)[..., None]
    half_rows = plane_count * orders_each * 2
    synth = np.stack([cosine * factor, -sine * factor], axis=3)
    synth = synth.reshape(2, half_rows, lon_count).astype(ml_dtypes.bfloat16)
    analysis = np.stack([cosine, -sine], axis=3)
    analysis = analysis.reshape(2, plane_count, orders_each // 2, 4, lon_count)
    analysis = analysis.transpose(0, 4, 2, 1, 3).reshape(2, lon_count, half_rows)
    return (jnp.asarray(synth), jnp.asarray(analysis.astype(ml_dtypes.bfloat16)))


def legendre_fill(block, start_ref, order_ref, cosine_ref, rows_ref, table_ref):
    degree_count = rows_ref.shape[0]
    order_f = order_ref[...]
    cosine = cosine_ref[...]
    zeros = jnp.zeros(cosine.shape, jnp.float32)

    def advance_block(step, state):
        older, newer, log_scale = state
        half_scale = jnp.exp(0.5 * log_scale)
        for offset in range(block):
            degree = step * block + offset
            degree_f = degree.astype(jnp.float32)
            below = degree_f - 1.0
            alpha_rec = jnp.sqrt(
                jnp.maximum(4.0 * degree_f * degree_f - 1.0, 1.0)
                / jnp.maximum(degree_f * degree_f - order_f * order_f, 1.0)
            )
            beta_rec = jnp.sqrt(
                jnp.maximum(below * below - order_f * order_f, 0.0)
                / jnp.maximum(4.0 * below * below - 1.0, 1.0)
            )
            recurred = alpha_rec * (cosine * newer - beta_rec * older)
            fresh = jnp.where(
                degree_f < order_f, 0.0, jnp.where(degree_f == order_f, 1.0, recurred)
            )
            rows_ref[degree] = (fresh * half_scale) * half_scale
            older, newer = newer, fresh
        largest = jnp.maximum(jnp.abs(older), jnp.abs(newer))
        norm_value = jnp.where(largest > 0.0, largest, 1.0)
        return (older / norm_value, newer / norm_value, log_scale + jnp.log(norm_value))

    lax.fori_loop(0, degree_count // block, advance_block, (zeros, zeros, start_ref[...]))
    for slot in range(table_ref.shape[0]):
        table_ref[slot] = rows_ref[:, slot, :].astype(jnp.bfloat16)


def legendre_start(orders, angles, degree_count):
    order_count = orders.shape[0]
    padded = (order_count + 7) // 8 * 8
    orders = jnp.concatenate([orders, jnp.broadcast_to(orders[:1], (padded - order_count,))])
    order_f = orders.astype(jnp.float32)[:, None]
    factor_index = jnp.arange(1, degree_count + 1).astype(jnp.float32)
    ratios = jnp.log((2.0 * factor_index - 1.0) / (2.0 * factor_index))
    partial_log = jnp.sum(jnp.where(factor_index[None, :] <= order_f, ratios[None, :], 0.0), axis=1)
    start_log = (
        0.5 * jnp.log(order_f + 0.5)
        + 0.5 * partial_log[:, None]
        + order_f * jnp.log(jnp.sin(angles))[None, :]
    )
    shape = start_log.shape
    return (
        start_log,
        jnp.broadcast_to(order_f, shape),
        jnp.broadcast_to(jnp.cos(angles)[None, :], shape),
    )


def fused_kernel(
    grid_ref, saved_ref, target_ref, weight_ref, mix_ref, gain_ref, up_ref, down_ref,
    synth_ref, analysis_ref, start_ref, order_ref, cosine_ref, quad_ref,
    out_ref,
    own_target, send_points, recv_points, send_cot, cot_ref, slopes_ref, mixed_ref,
    gather_f32, zsend, zrecv, psend, precv, wave_f32, rows_ref, table_ref, wave_ref,
    rsend, rrecv, yown, zsend_back, zrecv_back,
    target_sem, point_ss, point_rs, cot_ss, cot_rs, z_ss, z_rs, p_ss, p_rs, r_ss, r_rs,
    zb_ss, zb_rs,
):
    row_count, lon_count, channels = saved_ref.shape
    member_count = recv_points.shape[0]
    part = lon_count // member_count
    plane_count = precv.shape[0]
    pair_count = precv.shape[1]
    piece = precv.shape[2]
    orders_each = table_ref.shape[0]
    keys_each = 2 * orders_each
    chunk_count = rrecv.shape[0]
    chunk_keys = keys_each // chunk_count
    chunk_span = plane_count * chunk_keys
    row_slots = 2 * row_count

    member = lax.axis_index("member")
    lat = lax.axis_index("lat")
    half = lat // plane_count
    spot = lat - half * plane_count
    partner = {"lat": lax.rem(lat + plane_count, 2 * plane_count)}

    def member_peer(step):
        return {"member": lax.rem(member + step, member_count)}

    def plane_spot(step):
        return lax.rem(spot + step, plane_count)

    def plane_peer(step):
        return {"lat": half * plane_count + plane_spot(step)}

    target_copy = pltpu.make_async_copy(
        target_ref.at[:, pl.ds(member * part, part), :], own_target, target_sem
    )
    target_copy.start()

    barrier = pltpu.get_barrier_semaphore()
    for step in range(1, member_count):
        pl.semaphore_signal(barrier, inc=1, device_id=member_peer(step), device_id_type=MESH)
    pl.semaphore_signal(barrier, inc=1, device_id=partner, device_id_type=MESH)

    def greet(step, carry):
        pl.semaphore_signal(barrier, inc=1, device_id=plane_peer(step), device_id_type=MESH)
        return carry

    lax.fori_loop(1, plane_count, greet, 0)
    pl.semaphore_wait(barrier, member_count - 1 + 1 + plane_count - 1)

    def point_copy(row, step):
        return pltpu.make_async_remote_copy(
            src_ref=send_points.at[step - 1, row],
            dst_ref=recv_points.at[member_count - step, row],
            send_sem=point_ss.at[row, step - 1],
            recv_sem=point_rs.at[row, step - 1],
            device_id=member_peer(step),
            device_id_type=MESH,
        )

    def cot_copy(row, step):
        return pltpu.make_async_remote_copy(
            src_ref=send_cot.at[step - 1, row],
            dst_ref=cot_ref.at[row, pl.ds(member * part, part), :],
            send_sem=cot_ss.at[row, step - 1],
            recv_sem=cot_rs.at[row, step - 1],
            device_id=member_peer(step),
            device_id_type=MESH,
        )

    def z_copy(row):
        return pltpu.make_async_remote_copy(
            src_ref=zsend.at[row],
            dst_ref=zrecv.at[row],
            send_sem=z_ss.at[row],
            recv_sem=z_rs.at[row],
            device_id=partner,
            device_id_type=MESH,
        )

    def p_copy(pair, step):
        return pltpu.make_async_remote_copy(
            src_ref=psend.at[pair, plane_spot(step)],
            dst_ref=precv.at[spot, pair],
            send_sem=p_ss.at[pair, step],
            recv_sem=p_rs.at[pair, step],
            device_id=plane_peer(step),
            device_id_type=MESH,
        )

    def r_copy(chunk, step):
        return pltpu.make_async_remote_copy(
            src_ref=rsend.at[chunk, plane_spot(step)],
            dst_ref=rrecv.at[chunk, spot],
            send_sem=r_ss.at[chunk, step],
            recv_sem=r_rs.at[chunk, step],
            device_id=plane_peer(step),
            device_id_type=MESH,
        )

    def zb_copy(chunk):
        return pltpu.make_async_remote_copy(
            src_ref=zsend_back.at[:, pl.ds(chunk * chunk_span, chunk_span), :],
            dst_ref=zrecv_back.at[:, pl.ds(chunk * chunk_span, chunk_span), :],
            send_sem=zb_ss.at[chunk],
            recv_sem=zb_rs.at[chunk],
            device_id=partner,
            device_id_type=MESH,
        )

    def forward_part(row, step):
        begin = pl.multiple_of(lax.rem(member + step, member_count) * part, part)
        hidden_pre = dot_nn(saved_ref[row, pl.ds(begin, part), :], up_ref[...])
        values, slopes = gelu_parts(hidden_pre)
        slopes_ref[row, pl.ds(begin, part), :] = slopes.astype(jnp.bfloat16)
        branch = dot_nn(values.astype(jnp.bfloat16), down_ref[...])
        summed = grid_ref[row, pl.ds(begin, part), :].astype(jnp.float32) + branch
        return summed.astype(jnp.bfloat16)

    def forward_row(row):
        def one(step, carry):
            send_points[step - 1, row] = forward_part(row, step)
            point_copy(row, step).start()
            return carry

        lax.fori_loop(1, member_count, one, 0)
        recv_points[0, row] = forward_part(row, 0)

    strip = 16 if part % 16 == 0 else part

    def loss_row(row):
        for step in range(1, member_count):
            point_copy(row, step).wait_recv()
        own_begin = pl.multiple_of(member * part, part)

        def one(index, carry):
            begin = pl.multiple_of(index * strip, strip)
            here = pl.ds(begin, strip)
            values = [
                recv_points[slot, row, here, :].astype(jnp.float32) for slot in range(member_count)
            ]
            totals = [jnp.zeros(values[0].shape, jnp.float32) for slot in range(member_count)]
            for first in range(member_count):
                for second in range(first + 1, member_count):
                    slope = slope_abs(values[first] - values[second])
                    totals[first] = totals[first] + slope
                    totals[second] = totals[second] - slope
            wanted = own_target[row, here, :].astype(jnp.float32)
            weights = weight_ref[row, here, :]
            for slot in range(member_count):
                term = weights * (
                    slope_abs(values[slot] - wanted) / member_count
                    - totals[slot] / (member_count * member_count)
                )
                if slot == 0:
                    spot_here = pl.ds(pl.multiple_of(own_begin + begin, strip), strip)
                    cot_ref[row, spot_here, :] = term.astype(jnp.bfloat16)
                else:
                    send_cot[slot - 1, row, here, :] = term.astype(jnp.bfloat16)
            return carry

        lax.fori_loop(0, part // strip, one, 0)
        for step in range(1, member_count):
            cot_copy(row, step).start()

    blocks, lane_width = gather_f32.shape[0], gather_f32.shape[2]

    def lanes_of(block):
        return slice(block * lane_width, (block + 1) * lane_width)

    def scatter_rows(first, count, stride, values):
        for block in range(blocks):
            gather_f32[block, pl.ds(first, count, stride=stride), :] = values[:, lanes_of(block)]

    def backward_row(row, own_slot):
        for step in range(1, member_count):
            cot_copy(row, step).wait_recv()

        def one(index, carry):
            here = pl.ds(pl.multiple_of(index * part, part), part)
            act_grad = dot_nt(cot_ref[row, here, :], down_ref[...])
            pre_grad = (act_grad * slopes_ref[row, here, :].astype(jnp.float32)).astype(jnp.bfloat16)
            mixed_ref[here, :] = dot_nt(pre_grad, up_ref[...]).astype(jnp.bfloat16)
            return carry

        lax.fori_loop(0, member_count, one, 0)
        other = dot_nn(synth_ref[1 - half], mixed_ref[...])
        zsend[row] = other.astype(jnp.bfloat16)
        z_copy(row).start()
        own = dot_nn(synth_ref[half], mixed_ref[...])
        scatter_rows(own_slot, own.shape[0], 2 * pair_rows, own)

    def plane_pair(pair):
        for inner in range(pair_rows):
            row = pair * pair_rows + inner
            z_copy(row).wait_recv()
            scatter_rows(
                pair_rows + inner, zrecv.shape[1], 2 * pair_rows, zrecv[row].astype(jnp.float32)
            )
        for block in range(blocks):
            psend[pair, :, :, lanes_of(block)] = (
                gather_f32[block].reshape(plane_count, piece, lane_width).astype(jnp.bfloat16)
            )

        def one(step, carry):
            p_copy(pair, step).start()
            return carry

        lax.fori_loop(1, plane_count, one, 0)
        precv[spot, pair] = psend[pair, spot]

    forward_row(0)
    forward_row(1)
    legendre_fill(
        math.gcd(rows_ref.shape[0], 16), start_ref, order_ref, cosine_ref, rows_ref, table_ref
    )
    target_copy.wait()
    for row in range(row_count):
        loss_row(row)
        if row + 2 < row_count:
            forward_row(row + 2)
        if row >= 1:
            backward_row(row - 1, (row - 1) % pair_rows)
            if row % pair_rows == 0:
                plane_pair(row // pair_rows - 1)
    backward_row(row_count - 1, (row_count - 1) % pair_rows)
    plane_pair(pair_count - 1)

    def await_plane(step, carry):
        for pair in range(pair_count):
            p_copy(pair, step).wait_recv()
        return carry

    lax.fori_loop(1, plane_count, await_plane, 0)

    group = pair_count * piece

    def widen(index, carry):
        here = pl.ds(pl.multiple_of(index * group, group), group)
        for block in range(blocks):
            wave_f32[block, here, :] = (
                precv[index, :, :, lanes_of(block)].reshape(group, lane_width).astype(jnp.float32)
            )
        return carry

    lax.fori_loop(0, plane_count, widen, 0)
    slots_each = 2 * pair_rows

    def spectral_chunk(chunk):
        def one_order(inner, carry):
            order = chunk * (chunk_keys // 2) + inner
            for phase in range(2):
                key = order * 2 + phase
                for pair in range(pair_count):
                    for slot in range(slots_each):
                        first = pair * piece + key * slots_each + slot
                        begin = (pair * slots_each + slot) * plane_count
                        for block in range(blocks):
                            lane_begin = phase * channels + block * lane_width
                            wave_ref[
                                begin : begin + plane_count, lane_begin : lane_begin + lane_width
                            ] = wave_f32[block, pl.ds(first, plane_count, stride=group), :].astype(
                                jnp.bfloat16
                            )
            degree_grad = dot_nn(table_ref[order], wave_ref[...])
            gained = (degree_grad * gain_ref[...]).astype(jnp.bfloat16)
            coeff_grad = jnp.concatenate(
                [
                    dot_nt(gained[:, :channels], mix_ref[...]).astype(jnp.bfloat16),
                    dot_nt(gained[:, channels:], mix_ref[...]).astype(jnp.bfloat16),
                ],
                axis=1,
            )
            lat_grad = dot_tn(table_ref[order], coeff_grad) * quad_ref[...]
            for phase in range(2):
                for slot in range(row_slots):
                    first = (inner * 2 + phase) * row_slots + slot
                    scatter_rows(
                        first,
                        plane_count,
                        piece,
                        lat_grad[
                            slot * plane_count : (slot + 1) * plane_count,
                            phase * channels : (phase + 1) * channels,
                        ],
                    )
            return carry

        lax.fori_loop(0, chunk_keys // 2, one_order, 0)
        for block in range(blocks):
            rsend[chunk, :, :, lanes_of(block)] = (
                gather_f32[block].reshape(plane_count, piece, lane_width).astype(jnp.bfloat16)
            )

        def one(step, carry):
            r_copy(chunk, step).start()
            return carry

        lax.fori_loop(1, plane_count, one, 0)
        rrecv[chunk, spot] = rsend[chunk, spot]

    def return_chunk(chunk):
        def await_one(step, carry):
            r_copy(chunk, step).wait_recv()
            return carry

        lax.fori_loop(1, plane_count, await_one, 0)
        for block in range(blocks):
            gather_f32[block] = (
                rrecv[chunk, :, :, lanes_of(block)]
                .reshape(plane_count * piece, lane_width)
                .astype(jnp.float32)
            )
        here = pl.ds(chunk * chunk_span, chunk_span)
        for row in range(row_count):
            slot = (row // pair_rows) * slots_each + row % pair_rows
            for block in range(blocks):
                zsend_back[row, here, lanes_of(block)] = gather_f32[
                    block, pl.ds(slot + pair_rows, chunk_span, stride=row_slots), :
                ].astype(jnp.bfloat16)
        zb_copy(chunk).start()
        for row in range(row_count):
            slot = (row // pair_rows) * slots_each + row % pair_rows
            for block in range(blocks):
                yown[row, here, lanes_of(block)] = gather_f32[
                    block, pl.ds(slot, chunk_span, stride=row_slots), :
                ].astype(jnp.bfloat16)

    spectral_chunk(0)
    for chunk in range(1, chunk_count):
        spectral_chunk(chunk)
        return_chunk(chunk - 1)
    return_chunk(chunk_count - 1)
    for chunk in range(chunk_count):
        zb_copy(chunk).wait_recv()

    def finish(row, carry):
        spatial = dot_nn(analysis_ref[half], yown[row]) + dot_nn(
            analysis_ref[1 - half], zrecv_back[row]
        )
        out_ref[row] = (
            cot_ref[row].astype(jnp.float32) + spatial * (1.0 / lon_count)
        ).astype(jnp.bfloat16)
        return carry

    lax.fori_loop(0, row_count, finish, 0)

    def drain_rows(row, carry):
        for step in range(1, member_count):
            point_copy(row, step).wait_send()
            cot_copy(row, step).wait_send()
        z_copy(row).wait_send()
        return carry

    lax.fori_loop(0, row_count, drain_rows, 0)

    def drain_plane(step, carry):
        for pair in range(pair_count):
            p_copy(pair, step).wait_send()
        for chunk in range(chunk_count):
            r_copy(chunk, step).wait_send()
        return carry

    lax.fori_loop(1, plane_count, drain_plane, 0)
    for chunk in range(chunk_count):
        zb_copy(chunk).wait_send()


def shards(
    grid_input, saved_mixed, target, land_weight, mix_weight, degree_gain, up_weight, down_weight
):
    row_count, lon_count, channels = grid_input.shape[1:]
    hidden = up_weight.shape[1]
    total_lat = degree_gain.shape[0]
    member_count = lax.axis_size("member")
    plane_count = lax.axis_size("lat") // 2
    part = lon_count // member_count
    mode_count = lon_count // 2
    orders_each = mode_count // (2 * plane_count)
    pair_count = row_count // pair_rows
    chunk_count = orders_each // 2
    half_rows = mode_count
    piece = 2 * pair_rows * 2 * orders_each
    member = lax.axis_index("member")
    lat = lax.axis_index("lat")
    half = lat // plane_count
    spot = lat % plane_count

    local_angles = ((lat * row_count + jnp.arange(row_count)).astype(jnp.float32) + 0.5) * (
        math.pi / total_lat
    )
    own_land = lax.dynamic_slice_in_dim(land_weight, member * part, part, 1)
    weights = (jnp.sin(local_angles)[:, None] * own_land.astype(jnp.float32))[:, :, None]

    pair_index = jnp.arange(pair_count)[:, None, None, None]
    side = jnp.arange(2)[None, :, None, None]
    inner = jnp.arange(pair_rows)[None, None, :, None]
    sender = jnp.arange(plane_count)[None, None, None, :]
    side_half = jnp.where(side == 0, half, 1 - half)
    lat_rows = (
        (side_half * plane_count + sender) * row_count + pair_index * pair_rows + inner
    ).reshape(-1)
    angles = (lat_rows.astype(jnp.float32) + 0.5) * (math.pi / total_lat)
    quad_weight = jnp.sin(angles) * (math.pi / total_lat)
    orders = half * (mode_count // 2) + spot * orders_each + jnp.arange(orders_each)
    start_log, order_f, cosine = legendre_start(orders, angles, total_lat)
    synth, analysis = fourier_tables(lon_count, plane_count, orders_each)

    blocks = max(channels // 128, 1)
    bf16 = jnp.bfloat16
    f32 = jnp.float32
    vmem = pl.BlockSpec(memory_space=pltpu.VMEM)
    anywhere = pl.BlockSpec(memory_space=pl.ANY)
    dma = pltpu.SemaphoreType.DMA
    result = pl.pallas_call(
        fused_kernel,
        out_shape=jax.ShapeDtypeStruct((row_count, lon_count, channels), bf16),
        in_specs=[vmem, vmem, anywhere] + [vmem] * 11,
        out_specs=vmem,
        scratch_shapes=[
            pltpu.VMEM((row_count, part, channels), bf16),
            pltpu.VMEM((member_count - 1, row_count, part, channels), bf16),
            pltpu.VMEM((member_count, row_count, part, channels), bf16),
            pltpu.VMEM((member_count - 1, row_count, part, channels), bf16),
            pltpu.VMEM((row_count, lon_count, channels), bf16),
            pltpu.VMEM((row_count, lon_count, hidden), bf16),
            pltpu.VMEM((lon_count, channels), bf16),
            pltpu.VMEM((blocks, plane_count * piece, channels // blocks), f32),
            pltpu.VMEM((row_count, half_rows, channels), bf16),
            pltpu.VMEM((row_count, half_rows, channels), bf16),
            pltpu.VMEM((pair_count, plane_count, piece, channels), bf16),
            pltpu.VMEM((plane_count, pair_count, piece, channels), bf16),
            pltpu.VMEM((blocks, plane_count * pair_count * piece, channels // blocks), f32),
            pltpu.VMEM((total_lat,) + start_log.shape, f32),
            pltpu.VMEM((orders_each, total_lat, total_lat), bf16),
            pltpu.VMEM((total_lat, 2 * channels), bf16),
            pltpu.VMEM((chunk_count, plane_count, piece, channels), bf16),
            pltpu.VMEM((chunk_count, plane_count, piece, channels), bf16),
            pltpu.VMEM((row_count, half_rows, channels), bf16),
            pltpu.VMEM((row_count, half_rows, channels), bf16),
            pltpu.VMEM((row_count, half_rows, channels), bf16),
            dma,
            dma((row_count, member_count - 1)),
            dma((row_count, member_count - 1)),
            dma((row_count, member_count - 1)),
            dma((row_count, member_count - 1)),
            dma((row_count,)),
            dma((row_count,)),
            dma((pair_count, plane_count)),
            dma((pair_count, plane_count)),
            dma((chunk_count, plane_count)),
            dma((chunk_count, plane_count)),
            dma((chunk_count,)),
            dma((chunk_count,)),
        ],
        compiler_params=pltpu.CompilerParams(
            collective_id=0, has_side_effects=True, vmem_limit_bytes=62 * 2**20
        ),
    )(
        grid_input[0],
        saved_mixed[0],
        target,
        weights,
        mix_weight,
        degree_gain[:, None],
        up_weight,
        down_weight,
        synth,
        analysis,
        start_log,
        order_f,
        cosine,
        quad_weight[:, None],
    )
    return result[None]


def solution(mesh):
    in_specs = (
        P("member", "lat", None, None),
        P("member", "lat", None, None),
        P("lat", None, None),
        P("lat", None),
        P(),
        P(),
        P(),
        P(),
    )
    out_specs = P("member", "lat", None, None)
    return jax.shard_map(shards, mesh=mesh, in_specs=in_specs, out_specs=out_specs, check_vma=False)
```

time: 322 us -> 278 us (0.86)
  Pallas kernels: 8.92 us -> 268 us
  waiting for transfers between devices: 187 us -> 0 us
  matrix products: 37.4 us -> 0 us
  starting transfers between devices: 35.5 us -> 0 us
  local copies, waits for them, and re-layouts: 32.3 us -> 8.08 us
  other arithmetic: 17.9 us -> 2.06 us
    pallas_call x1, Pallas kernels: 8.92 us -> 268 us  [shards(): pl.pallas_call(fused_kernel, out_shape=jax.ShapeDtypeStruct((row_count, l...]
    all_to_all x4 -> x0, waiting for transfers between devices: 187 us -> none  [the longest x1 50.7 us: shards(): lax.all_to_all(member_out.reshape(rows_lat, member_count, part, channel_c...]
    dot_general x7 -> x0, matrix products: 37.4 us -> none  [the longest x1 10.4 us: shards(): jnp.dot(pre_grad, up_weight.T, preferred_element_type=jnp.float32)]
    all_to_all x4 -> x0, starting transfers between devices: 35.5 us -> none  [the longest x1 13.7 us: shards(): lax.all_to_all(wave_grad, 'lat', split_axis=2, concat_axis=0, tiled=True)]
    another operation x4 -> x0, other arithmetic: 16.6 us -> none
    all_to_all x3 -> x0, local copies, waits for them, and re-layouts: 11.9 us -> none  [the longest x1 4.74 us: shards(): lax.all_to_all(wave_grad, 'lat', split_axis=2, concat_axis=0, tiled=True)]
    reshape x2 -> x0, local copies, waits for them, and re-layouts: 9.03 us -> none  [the longest x1 5.18 us: shards(): returned.reshape(rows_lat, 2 * mode_count, channel_count)]
    convert_element_type x1 -> x0, local copies, waits for them, and re-layouts: 6.81 us -> none  [shards(): lat_grad = lat_grad.astype(jnp.bfloat16)]
  transfers between devices with their start and end apart: 4 -> 0, of which waited for: 4 -> 0; matrix products, arithmetic and copies ran while one was open for 4% -> 0% of each run, Pallas kernels for 3% -> 0%
where the time goes in v2:
time: 278 us
  Pallas kernels  268 us (96%)
  local copies, waits for them, and re-layouts  8.08 us (3%)
    pallas_call x1, Pallas kernels, shards(): pl.pallas_call(fused_kernel, out_shape=jax.ShapeDtypeStruct((row_count, l...  268 us

profile of v2, /device:TPU:102, one launch (start us, length us, event | category | flops | bytes accessed | tf_op | source)
XLA Modules:
  0.0 278.0 jit_solution(1897034966870323620)
XLA Ops:
  0.1 0.1 add_multiply_fusion.1
  0.2 0.1 broadcast_add_fusion
  0.3 0.2 select_reduce_fusion
  0.5 0.1 add_multiply_fusion.2
  0.5 0.8 multiply_bitcast_fusion
  1.3 0.7 le.14.order_ref
  2.0 0.1 fusion.2
  2.1 0.1 reshape.141
  2.2 0.1 reshape.139
  2.3 0.7 multiply_add_fusion.start_ref
  2.9 0.6 broadcast_in_dim.61.cosine_ref
  3.5 0.9 reshape.144.quad_ref
  4.4 1.5 broadcast_in_dim.63.gain_ref
  5.9 1.1 copy.11.weight_ref
  6.9 267.9 %shard_map.100 = bf16[6,768,256]{2,1,0:T(8,128)(2,1)} custom-call(bf16[6,768,256]{2,1,0:T(8,128)(2,1)} %bitcast.8, bf16[6,768,256]{2,1,0:T(8,128)(2,1)} %bitcast.9, bf16[6,768,256]{2,1,0:T(8,128)(2,1)} %target_ref.1, f32[6,192,1]{2,1,0:T(8,128)} %copy.11.weight_ref, bf16[256,256]{1,0:T(8,128)(2,1)} %mix_ref.1, f32[384,1]{1,0:T(8,128)} %broadcast_in_dim.63.gain_ref, ...), custom_call_target="tpu_custom_call" | custom-call | tf_op jit(solution)/shard_map/pallas_call | solution.py:541
  274.8 3.2 %copy.15 = bf16[1,6,768,256]{3,2,1,0:T(8,128)(2,1)} copy(bf16[1,6,768,256]{3,2,1,0:T(8,128)(2,1)} %bitcast.7) | data formatting | bytes 4718592
  (7 shorter events, 0.1 us)

commit v3 on v2

v3 whole, which is shorter than its diff:
```python
import functools
import math

import jax
import jax.numpy as jnp
import ml_dtypes
import numpy as np
from jax import lax
from jax.experimental import pallas as pl
from jax.experimental.pallas import tpu as pltpu
from jax.sharding import PartitionSpec as P

kappa_gelu = 0.7978845608
cubic_gelu = 0.044715
smooth_square = 0.25
pair_rows = 2
low_each = 4
high_each = 4
low_chunks = 2
MESH = pl.DeviceIdType.MESH


def gelu_parts(inputs):
    squared = inputs * inputs
    tanh_part = jnp.tanh(kappa_gelu * inputs * (1.0 + cubic_gelu * squared))
    half_sum = 0.5 * (1.0 + tanh_part)
    values = inputs * half_sum
    slopes = half_sum + 0.5 * inputs * (1.0 - tanh_part * tanh_part) * (
        kappa_gelu + (3.0 * cubic_gelu * kappa_gelu) * squared
    )
    return (values, slopes)


def slope_abs(difference):
    return difference * lax.rsqrt(difference * difference + smooth_square)


def dot_nn(lhs, rhs):
    return lax.dot_general(lhs, rhs, (((1,), (0,)), ((), ())), preferred_element_type=jnp.float32)


def dot_nt(lhs, rhs):
    return lax.dot_general(lhs, rhs, (((1,), (1,)), ((), ())), preferred_element_type=jnp.float32)


def dot_tn(lhs, rhs):
    return lax.dot_general(lhs, rhs, (((0,), (0,)), ((), ())), preferred_element_type=jnp.float32)


def orders_low(plane_count):
    return np.arange(2 * plane_count * low_each).reshape(2, plane_count, low_each)


def orders_high(plane_count):
    first = 2 * plane_count * low_each
    return first + np.arange(high_each)[None, :] * plane_count + np.arange(plane_count)[:, None]


def fourier_tables(lon_count, plane_count):
    positions = np.arange(lon_count)

    def entries(orders):
        phase = (orders[..., None] * positions) % lon_count
        angles = phase.astype(np.float32) * np.float32(2.0 * math.pi / lon_count)
        factor = np.where(orders == 0, 1.0, 2.0).astype(np.float32)[..., None]
        plain = np.stack([np.cos(angles), -np.sin(angles)], axis=-2)
        return (plain * factor[..., None], plain)

    low = orders_low(plane_count)
    high = orders_high(plane_count)
    rows = plane_count * low_each * 2
    low_synth, low_plain = entries(low)
    high_synth, high_plain = entries(high)
    synth = np.concatenate(
        [low_synth.reshape(2, rows, lon_count), high_synth.reshape(1, rows, lon_count)]
    )
    low_plain = low_plain.reshape(2, plane_count, low_chunks, -1, lon_count)
    low_plain = low_plain.transpose(0, 2, 1, 3, 4).reshape(2, rows, lon_count)
    analysis = np.concatenate([low_plain, high_plain.reshape(1, rows, lon_count)])
    analysis = analysis.transpose(0, 2, 1)
    return (
        jnp.asarray(synth.astype(ml_dtypes.bfloat16)),
        jnp.asarray(analysis.astype(ml_dtypes.bfloat16)),
    )


def latitude_tables(row_count, plane_count, total_lat):
    half = np.arange(2)[:, None, None, None]
    side = np.arange(2)[None, :, None, None]
    row = np.arange(row_count)[None, None, :, None]
    sender = np.arange(plane_count)[None, None, None, :]
    side_half = np.where(side == 0, half, 1 - half)
    lat_rows = ((side_half * plane_count + sender) * row_count + row).reshape(2, total_lat)
    angles = (lat_rows + 0.5) * (math.pi / total_lat)
    low = orders_low(plane_count)
    high = np.broadcast_to(orders_high(plane_count)[None], (2, plane_count, high_each))
    orders = np.concatenate([low, high], axis=2)
    factor_index = np.arange(1, total_lat + 1)
    ratios = np.log((2.0 * factor_index - 1.0) / (2.0 * factor_index))
    partial_log = np.concatenate([[0.0], np.cumsum(ratios)])[orders]
    start_log = (0.5 * np.log(orders + 0.5) + 0.5 * partial_log)[..., None] + orders[
        ..., None
    ] * np.log(np.sin(angles))[:, None, None, :]
    start_log = start_log.reshape(2 * plane_count, low_each + high_each, total_lat)
    cosine = np.broadcast_to(np.cos(angles)[:, None, :], (2, low_each + high_each, total_lat))
    quad = np.sin(angles) * (math.pi / total_lat)
    quad = np.broadcast_to(quad[:, :, None], (2, total_lat, 128))
    local = (np.arange(total_lat).reshape(2 * plane_count, row_count) + 0.5) * (math.pi / total_lat)
    area = np.zeros((2 * plane_count, 8, 128))
    area[:, :row_count, :] = np.sin(local)[:, :, None]
    return tuple(jnp.asarray(table.astype(np.float32)) for table in (start_log, cosine, quad, area))


def legendre_fill(block, start_ref, order_f, cosine_ref, rows_ref, table_ref, high_ref):
    degree_count = rows_ref.shape[0]
    cosine = cosine_ref[...]
    zeros = jnp.zeros(cosine.shape, jnp.float32)

    def advance_block(step, state):
        older, newer, log_scale = state
        half_scale = jnp.exp(0.5 * log_scale)
        for offset in range(block):
            degree = step * block + offset
            degree_f = degree.astype(jnp.float32)
            below = degree_f - 1.0
            alpha_rec = jnp.sqrt(
                jnp.maximum(4.0 * degree_f * degree_f - 1.0, 1.0)
                / jnp.maximum(degree_f * degree_f - order_f * order_f, 1.0)
            )
            beta_rec = jnp.sqrt(
                jnp.maximum(below * below - order_f * order_f, 0.0)
                / jnp.maximum(4.0 * below * below - 1.0, 1.0)
            )
            recurred = alpha_rec * (cosine * newer - beta_rec * older)
            fresh = jnp.where(
                degree_f < order_f, 0.0, jnp.where(degree_f == order_f, 1.0, recurred)
            )
            rows_ref[degree] = (fresh * half_scale) * half_scale
            older, newer = newer, fresh
        largest = jnp.maximum(jnp.abs(older), jnp.abs(newer))
        norm_value = jnp.where(largest > 0.0, largest, 1.0)
        return (older / norm_value, newer / norm_value, log_scale + jnp.log(norm_value))

    lax.fori_loop(0, degree_count // block, advance_block, (zeros, zeros, start_ref[...]))
    for slot in range(low_each):
        table_ref[slot] = rows_ref[:, slot, :].astype(jnp.bfloat16)
    for slot in range(high_each):
        kept = rows_ref[degree_count - high_ref.shape[1] :, low_each + slot, :]
        high_ref[slot] = kept[:, : high_ref.shape[2]].astype(jnp.bfloat16)


def fused_kernel(
    grid_ref, saved_ref, target_ref, land_ref, mix_ref, gain_ref, up_ref, down_ref,
    synth_ref, analysis_ref, start_all, cosine_all, quad_all, area_all,
    out_ref,
    own_target, start_ref, cosine_ref, quad_ref, area_ref, weight_rows, weight_ref, gain_low,
    gain_high,
    send_points, recv_points, send_cot, cot_ref, slopes_ref, mixed_ref,
    gather_f32, gather_high, zsend, zrecv, psend, precv, wave_f32, rows_ref, table_ref, high_ref,
    wave_ref, high_f32, high_send, high_recv, high_coeff, total_ref,
    rsend, rrecv, yown, yhigh, zsend_back, zrecv_back,
    local_sem, point_ss, point_rs, cot_ss, cot_rs, z_ss, z_rs, p_ss, p_rs, r_ss, r_rs,
    zb_ss, zb_rs, h_ss, h_rs,
):
    row_count, lon_count, channels = saved_ref.shape
    member_count = recv_points.shape[0]
    part = lon_count // member_count
    plane_count = precv.shape[0]
    pair_count = precv.shape[1]
    piece = precv.shape[2]
    chunk_count = rrecv.shape[0]
    chunk_orders = low_each // low_chunks
    chunk_span = plane_count * 2 * chunk_orders
    row_slots = 2 * row_count
    own_lats = row_count * plane_count
    total_lat = 2 * own_lats
    low_piece = 2 * low_each * 2 * pair_rows
    region = (high_each + 1) * plane_count

    member = lax.axis_index("member")
    lat = lax.axis_index("lat")
    half = lat // plane_count
    spot = lat - half * plane_count
    partner = {"lat": lax.rem(lat + plane_count, 2 * plane_count)}

    def member_peer(step):
        return {"member": lax.rem(member + step, member_count)}

    def plane_spot(step):
        return lax.rem(spot + step, plane_count)

    def plane_peer(step):
        return {"lat": half * plane_count + plane_spot(step)}

    local_copies = [
        pltpu.make_async_copy(
            target_ref.at[:, pl.ds(member * part, part), :], own_target, local_sem.at[0]
        ),
        pltpu.make_async_copy(start_all.at[lat], start_ref, local_sem.at[1]),
        pltpu.make_async_copy(cosine_all.at[half], cosine_ref, local_sem.at[2]),
        pltpu.make_async_copy(quad_all.at[half], quad_ref, local_sem.at[3]),
        pltpu.make_async_copy(area_all.at[lat], area_ref, local_sem.at[4]),
    ]
    for copy in local_copies:
        copy.start()

    barrier = pltpu.get_barrier_semaphore()
    for step in range(1, member_count):
        pl.semaphore_signal(barrier, inc=1, device_id=member_peer(step), device_id_type=MESH)
    pl.semaphore_signal(barrier, inc=1, device_id=partner, device_id_type=MESH)

    def greet(step, carry):
        pl.semaphore_signal(barrier, inc=1, device_id=plane_peer(step), device_id_type=MESH)
        return carry

    lax.fori_loop(1, plane_count, greet, 0)
    pl.semaphore_wait(barrier, member_count - 1 + 1 + plane_count - 1)

    def point_copy(row, step):
        return pltpu.make_async_remote_copy(
            src_ref=send_points.at[step - 1, row],
            dst_ref=recv_points.at[member_count - step, row],
            send_sem=point_ss.at[row, step - 1],
            recv_sem=point_rs.at[row, step - 1],
            device_id=member_peer(step),
            device_id_type=MESH,
        )

    def cot_copy(row, step):
        return pltpu.make_async_remote_copy(
            src_ref=send_cot.at[step - 1, row],
            dst_ref=cot_ref.at[row, pl.ds(member * part, part), :],
            send_sem=cot_ss.at[row, step - 1],
            recv_sem=cot_rs.at[row, step - 1],
            device_id=member_peer(step),
            device_id_type=MESH,
        )

    def z_copy(row):
        return pltpu.make_async_remote_copy(
            src_ref=zsend.at[row],
            dst_ref=zrecv.at[row],
            send_sem=z_ss.at[row],
            recv_sem=z_rs.at[row],
            device_id=partner,
            device_id_type=MESH,
        )

    def p_copy(pair, step):
        return pltpu.make_async_remote_copy(
            src_ref=psend.at[pair, plane_spot(step)],
            dst_ref=precv.at[spot, pair],
            send_sem=p_ss.at[pair, step],
            recv_sem=p_rs.at[pair, step],
            device_id=plane_peer(step),
            device_id_type=MESH,
        )

    def r_copy(chunk, step):
        return pltpu.make_async_remote_copy(
            src_ref=rsend.at[chunk, plane_spot(step)],
            dst_ref=rrecv.at[chunk, spot],
            send_sem=r_ss.at[chunk, step],
            recv_sem=r_rs.at[chunk, step],
            device_id=plane_peer(step),
            device_id_type=MESH,
        )

    def zb_copy(chunk):
        return pltpu.make_async_remote_copy(
            src_ref=zsend_back.at[:, pl.ds(chunk * chunk_span, chunk_span), :],
            dst_ref=zrecv_back.at[:, pl.ds(chunk * chunk_span, chunk_span), :],
            send_sem=zb_ss.at[chunk],
            recv_sem=zb_rs.at[chunk],
            device_id=partner,
            device_id_type=MESH,
        )

    def forward_part(row, step):
        begin = pl.multiple_of(lax.rem(member + step, member_count) * part, part)
        hidden_pre = dot_nn(saved_ref[row, pl.ds(begin, part), :], up_ref[...])
        values, slopes = gelu_parts(hidden_pre)
        slopes_ref[row, pl.ds(begin, part), :] = slopes.astype(jnp.bfloat16)
        branch = dot_nn(values.astype(jnp.bfloat16), down_ref[...])
        summed = grid_ref[row, pl.ds(begin, part), :].astype(jnp.float32) + branch
        return summed.astype(jnp.bfloat16)

    def forward_row(row):
        def one(step, carry):
            send_points[step - 1, row] = forward_part(row, step)
            point_copy(row, step).start()
            return carry

        lax.fori_loop(1, member_count, one, 0)
        recv_points[0, row] = forward_part(row, 0)

    def high_copy():
        theirs = pl.ds(pl.multiple_of((1 - half) * region, region), region)
        return pltpu.make_async_remote_copy(
            src_ref=high_send.at[theirs, :],
            dst_ref=high_recv,
            send_sem=h_ss.at[0],
            recv_sem=h_rs.at[0],
            device_id=partner,
            device_id_type=MESH,
        )

    def coeff_copy():
        mine = pl.ds(pl.multiple_of(half * region, region), region)
        return pltpu.make_async_remote_copy(
            src_ref=high_coeff.at[mine, :],
            dst_ref=high_coeff.at[mine, :],
            send_sem=h_ss.at[1],
            recv_sem=h_rs.at[1],
            device_id=partner,
            device_id_type=MESH,
        )

    strip = 16 if part % 16 == 0 else part

    def loss_row(row):
        for step in range(1, member_count):
            point_copy(row, step).wait_recv()
        own_begin = pl.multiple_of(member * part, part)

        def one(index, carry):
            begin = pl.multiple_of(index * strip, strip)
            here = pl.ds(begin, strip)
            values = [
                recv_points[slot, row, here, :].astype(jnp.float32) for slot in range(member_count)
            ]
            totals = [jnp.zeros(values[0].shape, jnp.float32) for slot in range(member_count)]
            for first in range(member_count):
                for second in range(first + 1, member_count):
                    slope = slope_abs(values[first] - values[second])
                    totals[first] = totals[first] + slope
                    totals[second] = totals[second] - slope
            wanted = own_target[row, here, :].astype(jnp.float32)
            spot_here = pl.ds(pl.multiple_of(own_begin + begin, strip), strip)
            weights = weight_ref[spot_here, row : row + 1]
            for slot in range(member_count):
                term = weights * (
                    slope_abs(values[slot] - wanted) / member_count
                    - totals[slot] / (member_count * member_count)
                )
                if slot == 0:
                    cot_ref[row, spot_here, :] = term.astype(jnp.bfloat16)
                else:
                    send_cot[slot - 1, row, here, :] = term.astype(jnp.bfloat16)
            return carry

        lax.fori_loop(0, part // strip, one, 0)
        for step in range(1, member_count):
            cot_copy(row, step).start()

    blocks, lane_width = gather_f32.shape[0], gather_f32.shape[2]

    def lanes_of(block):
        return slice(block * lane_width, (block + 1) * lane_width)

    def scatter_rows(target, first, count, stride, values):
        for block in range(blocks):
            target[block, pl.ds(first, count, stride=stride), :] = values[:, lanes_of(block)]

    def backward_row(row, own_slot):
        for step in range(1, member_count):
            cot_copy(row, step).wait_recv()

        def one(index, carry):
            here = pl.ds(pl.multiple_of(index * part, part), part)
            act_grad = dot_nt(cot_ref[row, here, :], down_ref[...])
            pre_grad = (act_grad * slopes_ref[row, here, :].astype(jnp.float32)).astype(jnp.bfloat16)
            mixed_ref[here, :] = dot_nt(pre_grad, up_ref[...]).astype(jnp.bfloat16)
            return carry

        lax.fori_loop(0, member_count, one, 0)
        other = dot_nn(synth_ref[1 - half], mixed_ref[...])
        zsend[row] = other.astype(jnp.bfloat16)
        z_copy(row).start()
        own = dot_nn(synth_ref[half], mixed_ref[...])
        scatter_rows(gather_f32, own_slot, own.shape[0], 2 * pair_rows, own)
        high = dot_nn(synth_ref[2], mixed_ref[...])
        scatter_rows(gather_high, own_slot, high.shape[0], pair_rows, high)

    def plane_pair(pair):
        for inner in range(pair_rows):
            row = pair * pair_rows + inner
            z_copy(row).wait_recv()
            scatter_rows(
                gather_f32,
                pair_rows + inner,
                zrecv.shape[1],
                2 * pair_rows,
                zrecv[row].astype(jnp.float32),
            )
        for block in range(blocks):
            psend[pair, :, :low_piece, lanes_of(block)] = (
                gather_f32[block, : plane_count * low_piece]
                .reshape(plane_count, low_piece, lane_width)
                .astype(jnp.bfloat16)
            )
            psend[pair, :, low_piece:, lanes_of(block)] = (
                gather_high[block]
                .reshape(plane_count, piece - low_piece, lane_width)
                .astype(jnp.bfloat16)
            )

        def one(step, carry):
            p_copy(pair, step).start()
            return carry

        lax.fori_loop(1, plane_count, one, 0)
        precv[spot, pair] = psend[pair, spot]

    group = pair_count * piece

    def await_pair(pair):
        def one(step, carry):
            p_copy(pair, step).wait_recv()
            return carry

        lax.fori_loop(1, plane_count, one, 0)

        def widen(index, carry):
            here = pl.ds(pl.multiple_of(index * group + pair * piece, piece), piece)
            for block in range(blocks):
                wave_f32[block, here, :] = precv[index, pair, :, lanes_of(block)].astype(
                    jnp.float32
                )
            return carry

        lax.fori_loop(0, plane_count, widen, 0)

    def collect(first, begin, phase):
        for block in range(blocks):
            lane_begin = phase * channels + block * lane_width
            wave_ref[begin : begin + plane_count, lane_begin : lane_begin + lane_width] = wave_f32[
                block, pl.ds(first, plane_count, stride=group), :
            ].astype(jnp.bfloat16)

    def mix(gained):
        return jnp.concatenate(
            [
                dot_nt(gained[:, :channels], mix_ref[...]).astype(jnp.bfloat16),
                dot_nt(gained[:, channels:], mix_ref[...]).astype(jnp.bfloat16),
            ],
            axis=1,
        )

    def send_chunk(chunk):
        for block in range(blocks):
            rsend[chunk, :, :, lanes_of(block)] = (
                gather_f32[block].reshape(plane_count, piece, lane_width).astype(jnp.bfloat16)
            )

        def one(step, carry):
            r_copy(chunk, step).start()
            return carry

        lax.fori_loop(1, plane_count, one, 0)
        rrecv[chunk, spot] = rsend[chunk, spot]

    def receive_chunk(chunk):
        def one(step, carry):
            r_copy(chunk, step).wait_recv()
            return carry

        lax.fori_loop(1, plane_count, one, 0)
        for block in range(blocks):
            gather_f32[block] = (
                rrecv[chunk, :, :, lanes_of(block)]
                .reshape(plane_count * piece, lane_width)
                .astype(jnp.float32)
            )

    def low_chunk(chunk):
        def one_order(inner, carry):
            order = chunk * chunk_orders + inner
            for phase in range(2):
                key = order * 2 + phase
                for side in range(2):
                    for row in range(row_count):
                        slot = side * pair_rows + row % pair_rows
                        first = (row // pair_rows) * piece + key * 2 * pair_rows + slot
                        collect(first, (side * row_count + row) * plane_count, phase)
            degree_grad = dot_nn(table_ref[order], wave_ref[...])
            coeff_grad = mix((degree_grad * gain_low[:, 0:1]).astype(jnp.bfloat16))
            lat_grad = dot_tn(table_ref[order], coeff_grad) * quad_ref[:, 0:1]
            for phase in range(2):
                for slot in range(row_slots):
                    scatter_rows(
                        gather_f32,
                        (inner * 2 + phase) * row_slots + slot,
                        plane_count,
                        piece,
                        lat_grad[
                            slot * plane_count : (slot + 1) * plane_count,
                            phase * channels : (phase + 1) * channels,
                        ],
                    )
            return carry

        lax.fori_loop(0, chunk_orders, one_order, 0)
        send_chunk(chunk)

    high_first = [0, 5 * plane_count, 8 * plane_count, 4 * plane_count]
    high_size = [(high_each - slot) * plane_count for slot in range(high_each)]

    def high_analysis():
        for slot in range(high_each):
            for phase in range(2):
                key = slot * 2 + phase
                for row in range(row_count):
                    first = (
                        (row // pair_rows) * piece
                        + low_piece
                        + key * pair_rows
                        + row % pair_rows
                    )
                    collect(first, row * plane_count, phase)
            here = slice(high_first[slot], high_first[slot] + high_size[slot])
            total = dot_nn(high_ref[slot, slot * plane_count :, :], wave_ref[:own_lats, :])
            high_f32[here, :] = total
            high_send[here, :] = total.astype(jnp.bfloat16)
        high_copy().start()

    def high_middle():
        high_copy().wait_recv()
        mine = pl.ds(pl.multiple_of(half * region, region), region)
        total = high_f32[mine, :] + high_recv[...].astype(jnp.float32)
        gained = (total * gain_high[mine, 0:1]).astype(jnp.bfloat16)
        high_coeff[mine, :] = mix(gained)
        coeff_copy().start()

    def high_synthesis():
        coeff_copy().wait_recv()
        for slot in range(high_each):
            here = slice(high_first[slot], high_first[slot] + high_size[slot])
            lat_grad = (
                dot_tn(high_ref[slot, slot * plane_count :, :], high_coeff[here, :])
                * quad_ref[:own_lats, 0:1]
            )
            for phase in range(2):
                for row in range(row_count):
                    scatter_rows(
                        gather_f32,
                        (slot * 2 + phase) * row_count + row,
                        plane_count,
                        piece,
                        lat_grad[
                            row * plane_count : (row + 1) * plane_count,
                            phase * channels : (phase + 1) * channels,
                        ],
                    )
        send_chunk(low_chunks)

    def return_low(chunk):
        receive_chunk(chunk)
        here = pl.ds(chunk * chunk_span, chunk_span)
        for row in range(row_count):
            for block in range(blocks):
                zsend_back[row, here, lanes_of(block)] = gather_f32[
                    block, pl.ds(row_count + row, chunk_span, stride=row_slots), :
                ].astype(jnp.bfloat16)
        zb_copy(chunk).start()
        for row in range(row_count):
            for block in range(blocks):
                yown[row, here, lanes_of(block)] = gather_f32[
                    block, pl.ds(row, chunk_span, stride=row_slots), :
                ].astype(jnp.bfloat16)

    def return_high():
        receive_chunk(low_chunks)
        for row in range(row_count):
            for block in range(blocks):
                yhigh[row, :, lanes_of(block)] = gather_f32[
                    block, pl.ds(row, yhigh.shape[1], stride=row_count), :
                ].astype(jnp.bfloat16)

    forward_row(0)
    forward_row(1)
    for copy in local_copies:
        copy.wait()
    spread = lax.broadcasted_iota(jnp.int32, cosine_ref.shape, 0)
    low_order = half * (plane_count * low_each) + spot * low_each + spread
    high_order = 2 * plane_count * low_each + (spread - low_each) * plane_count + spot
    order_f = jnp.where(spread < low_each, low_order, high_order).astype(jnp.float32)
    weight_rows[...] = jnp.zeros(weight_rows.shape, jnp.float32)
    weight_rows[:row_count, :] = land_ref[...].astype(jnp.float32) * area_ref[:row_count, 0:1]
    weight_ref[...] = weight_rows[...].T
    gain_low[...] = jnp.broadcast_to(gain_ref[...], (8, total_lat)).T
    for slot in range(high_each):
        gain_high[high_first[slot] : high_first[slot] + high_size[slot], :] = gain_low[
            total_lat - high_size[slot] :, :
        ]
    legendre_fill(
        math.gcd(total_lat, 16), start_ref, order_f, cosine_ref, rows_ref, table_ref, high_ref
    )
    for row in range(row_count):
        loss_row(row)
        if row + 2 < row_count:
            forward_row(row + 2)
        if row >= 1:
            backward_row(row - 1, (row - 1) % pair_rows)
            if row % pair_rows == 0:
                plane_pair(row // pair_rows - 1)
    backward_row(row_count - 1, (row_count - 1) % pair_rows)
    for pair in range(pair_count - 1):
        await_pair(pair)
    plane_pair(pair_count - 1)
    await_pair(pair_count - 1)

    high_analysis()
    low_chunk(0)
    high_middle()
    for chunk in range(1, low_chunks):
        low_chunk(chunk)
        return_low(chunk - 1)
    high_synthesis()
    return_low(low_chunks - 1)
    return_high()

    def own_part(row, carry):
        total_ref[row] = dot_nn(analysis_ref[half], yown[row]) + dot_nn(analysis_ref[2], yhigh[row])
        return carry

    lax.fori_loop(0, row_count, own_part, 0)
    for chunk in range(low_chunks):
        zb_copy(chunk).wait_recv()

    def finish(row, carry):
        spatial = total_ref[row] + dot_nn(analysis_ref[1 - half], zrecv_back[row])
        out_ref[row] = (
            cot_ref[row].astype(jnp.float32) + spatial * (1.0 / lon_count)
        ).astype(jnp.bfloat16)
        return carry

    lax.fori_loop(0, row_count, finish, 0)

    def drain_rows(row, carry):
        for step in range(1, member_count):
            point_copy(row, step).wait_send()
            cot_copy(row, step).wait_send()
        z_copy(row).wait_send()
        return carry

    lax.fori_loop(0, row_count, drain_rows, 0)

    def drain_plane(step, carry):
        for pair in range(pair_count):
            p_copy(pair, step).wait_send()
        for chunk in range(chunk_count):
            r_copy(chunk, step).wait_send()
        return carry

    lax.fori_loop(1, plane_count, drain_plane, 0)
    for chunk in range(low_chunks):
        zb_copy(chunk).wait_send()
    high_copy().wait_send()
    coeff_copy().wait_send()


def shards(
    grid_input, saved_mixed, target, land_weight, mix_weight, degree_gain, up_weight, down_weight
):
    row_count, lon_count, channels = grid_input.shape[1:]
    hidden = up_weight.shape[1]
    total_lat = degree_gain.shape[0]
    member_count = lax.axis_size("member")
    plane_count = lax.axis_size("lat") // 2
    part = lon_count // member_count
    pair_count = row_count // pair_rows
    chunk_count = low_chunks + 1
    keys = plane_count * 2 * low_each
    low_piece = 2 * low_each * 2 * pair_rows
    piece = low_piece + 2 * high_each * pair_rows
    order_slots = low_each + high_each
    region = (high_each + 1) * plane_count
    own_lats = row_count * plane_count
    synth, analysis = fourier_tables(lon_count, plane_count)
    start_log, cosine, quad, area = latitude_tables(row_count, plane_count, total_lat)

    blocks = max(channels // 128, 1)
    bf16 = jnp.bfloat16
    f32 = jnp.float32
    vmem = pl.BlockSpec(memory_space=pltpu.VMEM)
    anywhere = pl.BlockSpec(memory_space=pl.ANY)
    dma = pltpu.SemaphoreType.DMA
    result = pl.pallas_call(
        fused_kernel,
        out_shape=jax.ShapeDtypeStruct((row_count, lon_count, channels), bf16),
        in_specs=[vmem, vmem, anywhere] + [vmem] * 7 + [anywhere] * 4,
        out_specs=vmem,
        scratch_shapes=[
            pltpu.VMEM((row_count, part, channels), bf16),
            pltpu.VMEM((order_slots, total_lat), f32),
            pltpu.VMEM((order_slots, total_lat), f32),
            pltpu.VMEM((total_lat, 128), f32),
            pltpu.VMEM((8, 128), f32),
            pltpu.VMEM((8, lon_count), f32),
            pltpu.VMEM((lon_count, 8), f32),
            pltpu.VMEM((total_lat, 8), f32),
            pltpu.VMEM((2 * region, 8), f32),
            pltpu.VMEM((member_count - 1, row_count, part, channels), bf16),
            pltpu.VMEM((member_count, row_count, part, channels), bf16),
            pltpu.VMEM((member_count - 1, row_count, part, channels), bf16),
            pltpu.VMEM((row_count, lon_count, channels), bf16),
            pltpu.VMEM((row_count, lon_count, hidden), bf16),
            pltpu.VMEM((lon_count, channels), bf16),
            pltpu.VMEM((blocks, plane_count * piece, channels // blocks), f32),
            pltpu.VMEM((blocks, plane_count * (piece - low_piece), channels // blocks), f32),
            pltpu.VMEM((row_count, keys, channels), bf16),
            pltpu.VMEM((row_count, keys, channels), bf16),
            pltpu.VMEM((pair_count, plane_count, piece, channels), bf16),
            pltpu.VMEM((plane_count, pair_count, piece, channels), bf16),
            pltpu.VMEM((blocks, plane_count * pair_count * piece, channels // blocks), f32),
            pltpu.VMEM((total_lat, order_slots, total_lat), f32),
            pltpu.VMEM((low_each, total_lat, total_lat), bf16),
            pltpu.VMEM((high_each, high_each * plane_count, own_lats), bf16),
            pltpu.VMEM((total_lat, 2 * channels), bf16),
            pltpu.VMEM((2 * region, 2 * channels), f32),
            pltpu.VMEM((2 * region, 2 * channels), bf16),
            pltpu.VMEM((region, 2 * channels), bf16),
            pltpu.VMEM((2 * region, 2 * channels), bf16),
            pltpu.VMEM((row_count, lon_count, channels), f32),
            pltpu.VMEM((chunk_count, plane_count, piece, channels), bf16),
            pltpu.VMEM((chunk_count, plane_count, piece, channels), bf16),
            pltpu.VMEM((row_count, keys, channels), bf16),
            pltpu.VMEM((row_count, keys, channels), bf16),
            pltpu.VMEM((row_count, keys, channels), bf16),
            pltpu.VMEM((row_count, keys, channels), bf16),
            dma((5,)),
            dma((row_count, member_count - 1)),
            dma((row_count, member_count - 1)),
            dma((row_count, member_count - 1)),
            dma((row_count, member_count - 1)),
            dma((row_count,)),
            dma((row_count,)),
            dma((pair_count, plane_count)),
            dma((pair_count, plane_count)),
            dma((chunk_count, plane_count)),
            dma((chunk_count, plane_count)),
            dma((low_chunks,)),
            dma((low_chunks,)),
            dma((2,)),
            dma((2,)),
        ],
        compiler_params=pltpu.CompilerParams(
            collective_id=0, has_side_effects=True, vmem_limit_bytes=63 * 2**20
        ),
    )(
        grid_input[0],
        saved_mixed[0],
        target,
        land_weight,
        mix_weight,
        degree_gain[None, :],
        up_weight,
        down_weight,
        synth,
        analysis,
        start_log,
        cosine,
        quad,
        area,
    )
    return result[None]


def solution(mesh):
    in_specs = (
        P("member", "lat", None, None),
        P("member", "lat", None, None),
        P("lat", None, None),
        P("lat", None),
        P(),
        P(),
        P(),
        P(),
    )
    out_specs = P("member", "lat", None, None)
    return jax.shard_map(shards, mesh=mesh, in_specs=in_specs, out_specs=out_specs, check_vma=False)
```

time: 278 us -> 231 us (0.83)
  Pallas kernels: 268 us -> 225 us
  local copies, waits for them, and re-layouts: 8.08 us -> 4.47 us
    pallas_call x1, Pallas kernels: 268 us -> 225 us  [shards(): pl.pallas_call(fused_kernel, out_shape=jax.ShapeDtypeStruct((row_count, l...]
where the time goes in v3:
time: 231 us; the launch traced here: 229 us
  Pallas kernels  225 us (97%)
  local copies, waits for them, and re-layouts  4.47 us (2%)
    pallas_call x1, Pallas kernels, shards(): pl.pallas_call(fused_kernel, out_shape=jax.ShapeDtypeStruct((row_count, l...  225 us

profile of v3, /device:TPU:102, one launch (start us, length us, event | category | flops | bytes accessed | tf_op | source)
XLA Modules:
  0.0 229.1 jit_solution(6386069312947868744)
XLA Ops:
  0.0 1.2 broadcast_in_dim.6.gain_ref
  1.2 224.6 %shard_map.136 = bf16[6,768,256]{2,1,0:T(8,128)(2,1)} custom-call(bf16[6,768,256]{2,1,0:T(8,128)(2,1)} %bitcast.4, bf16[6,768,256]{2,1,0:T(8,128)(2,1)} %bitcast.5, bf16[6,768,256]{2,1,0:T(8,128)(2,1)} %target_ref.1, s32[6,768]{1,0:T(8,128)} %land_ref.1, bf16[256,256]{1,0:T(8,128)(2,1)} %mix_ref.1, f32[1,384]{1,0:T(1,128)} %broadcast_in_dim.6.gain_ref, ...), custom_call_target="tpu_custom_call" | custom-call | tf_op jit(solution)/shard_map/pallas_call | solution.py:689
  225.9 3.2 %copy.16 = bf16[1,6,768,256]{3,2,1,0:T(8,128)(2,1)} copy(bf16[1,6,768,256]{3,2,1,0:T(8,128)(2,1)} %bitcast.3) | data formatting | bytes 4718592

commit v4 on v3

--- a/solution.py
+++ b/solution.py
@@ -16,7 +16,6 @@
 pair_rows = 2
 low_each = 4
 high_each = 4
-low_chunks = 2
 MESH = pl.DeviceIdType.MESH
 
 
@@ -74,9 +73,9 @@
     synth = np.concatenate(
         [low_synth.reshape(2, rows, lon_count), high_synth.reshape(1, rows, lon_count)]
     )
-    low_plain = low_plain.reshape(2, plane_count, low_chunks, -1, lon_count)
-    low_plain = low_plain.transpose(0, 2, 1, 3, 4).reshape(2, rows, lon_count)
-    analysis = np.concatenate([low_plain, high_plain.reshape(1, rows, lon_count)])
+    analysis = np.concatenate(
+        [low_plain.reshape(2, rows, lon_count), high_plain.reshape(1, rows, lon_count)]
+    )
     analysis = analysis.transpose(0, 2, 1)
     return (
         jnp.asarray(synth.astype(ml_dtypes.bfloat16)),
@@ -150,16 +149,18 @@
 
 
 def fused_kernel(
-    grid_ref, saved_ref, target_ref, land_ref, mix_ref, gain_ref, up_ref, down_ref,
-    synth_ref, analysis_ref, start_all, cosine_all, quad_all, area_all,
-    out_ref,
+    grid_all, saved_all, target_ref, land_ref, mix_ref, gain_ref, up_ref, down_ref,
+    synth_all, analysis_all, start_all, cosine_all, quad_all, area_all,
+    out_all,
+    grid_ref, saved_ref, synth_ref, analysis_ref,
     own_target, start_ref, cosine_ref, quad_ref, area_ref, weight_rows, weight_ref, gain_low,
     gain_high,
     send_points, recv_points, send_cot, cot_ref, slopes_ref, mixed_ref,
-    gather_f32, gather_high, zsend, zrecv, psend, precv, wave_f32, rows_ref, table_ref, high_ref,
-    wave_ref, high_f32, high_send, high_recv, high_coeff, total_ref,
+    gather_own, gather_high, gather_other, gather_f32, gather_late,
+    zsend, zrecv, psend, precv, wave_f32, rows_ref, table_ref, high_ref,
+    wave_ref, coeff_ref, high_f32, high_send, high_recv, high_coeff, total_ref,
     rsend, rrecv, yown, yhigh, zsend_back, zrecv_back,
-    local_sem, point_ss, point_rs, cot_ss, cot_rs, z_ss, z_rs, p_ss, p_rs, r_ss, r_rs,
+    local_sem, row_sem, point_ss, point_rs, cot_ss, cot_rs, z_ss, z_rs, p_ss, p_rs, r_ss, r_rs,
     zb_ss, zb_rs, h_ss, h_rs,
 ):
     row_count, lon_count, channels = saved_ref.shape
@@ -168,13 +169,10 @@
     plane_count = precv.shape[0]
     pair_count = precv.shape[1]
     piece = precv.shape[2]
-    chunk_count = rrecv.shape[0]
-    chunk_orders = low_each // low_chunks
-    chunk_span = plane_count * 2 * chunk_orders
-    row_slots = 2 * row_count
+    third = piece // 3
+    keys = 2 * low_each
     own_lats = row_count * plane_count
     total_lat = 2 * own_lats
-    low_piece = 2 * low_each * 2 * pair_rows
     region = (high_each + 1) * plane_count
 
     member = lax.axis_index("member")
@@ -186,11 +184,39 @@
     def member_peer(step):
         return {"member": lax.rem(member + step, member_count)}
 
+    cores = 2
+    columns = min(4, plane_count // cores)
+    lines = plane_count // (cores * columns)
+
     def plane_spot(step):
-        return lax.rem(spot + step, plane_count)
+        shift = lax.rem(step * 19, plane_count)
+        core = lax.rem(spot + shift, cores)
+        column = lax.rem(spot // cores + shift // cores, columns)
+        line = lax.rem(spot // (cores * columns) + shift // (cores * columns), lines)
+        return (line * columns + column) * cores + core
 
     def plane_peer(step):
         return {"lat": half * plane_count + plane_spot(step)}
+
+    barrier = pltpu.get_barrier_semaphore()
+    for step in range(1, member_count):
+        pl.semaphore_signal(barrier, inc=1, device_id=member_peer(step), device_id_type=MESH)
+    pl.semaphore_signal(barrier, inc=1, device_id=partner, device_id_type=MESH)
+
+    def greet(step, carry):
+        pl.semaphore_signal(barrier, inc=1, device_id=plane_peer(step), device_id_type=MESH)
+        return carry
+
+    lax.fori_loop(1, plane_count, greet, 0)
+
+    def row_copies(row):
+        return [
+            pltpu.make_async_copy(saved_all.at[row], saved_ref.at[row], row_sem.at[0, row]),
+            pltpu.make_async_copy(grid_all.at[row], grid_ref.at[row], row_sem.at[1, row]),
+        ]
+
+    def out_copy(row):
+        return pltpu.make_async_copy(saved_ref.at[row], out_all.at[row], row_sem.at[2, row])
 
     local_copies = [
         pltpu.make_async_copy(
@@ -200,21 +226,14 @@
         pltpu.make_async_copy(cosine_all.at[half], cosine_ref, local_sem.at[2]),
         pltpu.make_async_copy(quad_all.at[half], quad_ref, local_sem.at[3]),
         pltpu.make_async_copy(area_all.at[lat], area_ref, local_sem.at[4]),
+        pltpu.make_async_copy(synth_all, synth_ref, local_sem.at[5]),
+        pltpu.make_async_copy(analysis_all, analysis_ref, local_sem.at[6]),
     ]
-    for copy in local_copies:
+    for copy in row_copies(0) + row_copies(1) + local_copies:
         copy.start()
-
-    barrier = pltpu.get_barrier_semaphore()
-    for step in range(1, member_count):
-        pl.semaphore_signal(barrier, inc=1, device_id=member_peer(step), device_id_type=MESH)
-    pl.semaphore_signal(barrier, inc=1, device_id=partner, device_id_type=MESH)
-
-    def greet(step, carry):
-        pl.semaphore_signal(barrier, inc=1, device_id=plane_peer(step), device_id_type=MESH)
-        return carry
-
-    lax.fori_loop(1, plane_count, greet, 0)
-    pl.semaphore_wait(barrier, member_count - 1 + 1 + plane_count - 1)
+    for row in range(2, row_count):
+        for copy in row_copies(row):
+            copy.start()
 
     def point_copy(row, step):
         return pltpu.make_async_remote_copy(
@@ -246,32 +265,38 @@
             device_id_type=MESH,
         )
 
-    def p_copy(pair, step):
+    def p_copy(pair, side, step):
+        rows = pl.ds(0, 2 * third) if side == 0 else pl.ds(2 * third, third)
         return pltpu.make_async_remote_copy(
-            src_ref=psend.at[pair, plane_spot(step)],
-            dst_ref=precv.at[spot, pair],
-            send_sem=p_ss.at[pair, step],
-            recv_sem=p_rs.at[pair, step],
+            src_ref=psend.at[pair, plane_spot(step), rows, :],
+            dst_ref=precv.at[spot, pair, rows, :],
+            send_sem=p_ss.at[pair, side, step],
+            recv_sem=p_rs.at[pair, side, step],
             device_id=plane_peer(step),
             device_id_type=MESH,
         )
 
-    def r_copy(chunk, step):
+    def r_copy(index, step):
+        if index < pair_count:
+            slot, rows = 0, pl.ds(index * third, third)
+        else:
+            slot, rows = index - pair_count + 1, pl.ds(0, piece)
         return pltpu.make_async_remote_copy(
-            src_ref=rsend.at[chunk, plane_spot(step)],
-            dst_ref=rrecv.at[chunk, spot],
-            send_sem=r_ss.at[chunk, step],
-            recv_sem=r_rs.at[chunk, step],
+            src_ref=rsend.at[slot, plane_spot(step), rows, :],
+            dst_ref=rrecv.at[slot, spot, rows, :],
+            send_sem=r_ss.at[index, step],
+            recv_sem=r_rs.at[index, step],
             device_id=plane_peer(step),
             device_id_type=MESH,
         )
 
-    def zb_copy(chunk):
+    def zb_copy(pair):
+        rows = pl.ds(pair * pair_rows, pair_rows)
         return pltpu.make_async_remote_copy(
-            src_ref=zsend_back.at[:, pl.ds(chunk * chunk_span, chunk_span), :],
-            dst_ref=zrecv_back.at[:, pl.ds(chunk * chunk_span, chunk_span), :],
-            send_sem=zb_ss.at[chunk],
-            recv_sem=zb_rs.at[chunk],
+            src_ref=zsend_back.at[rows],
+            dst_ref=zrecv_back.at[rows],
+            send_sem=zb_ss.at[pair],
+            recv_sem=zb_rs.at[pair],
             device_id=partner,
             device_id_type=MESH,
         )
@@ -291,8 +316,14 @@
             point_copy(row, step).start()
             return carry
 
+        for copy in row_copies(row):
+            copy.wait()
+        if row == 0:
+            recv_points[0, row] = forward_part(row, 0)
+            pl.semaphore_wait(barrier, member_count - 1 + 1 + plane_count - 1)
         lax.fori_loop(1, member_count, one, 0)
-        recv_points[0, row] = forward_part(row, 0)
+        if row > 0:
+            recv_points[0, row] = forward_part(row, 0)
 
     def high_copy():
         theirs = pl.ds(pl.multiple_of((1 - half) * region, region), region)
@@ -378,55 +409,56 @@
         zsend[row] = other.astype(jnp.bfloat16)
         z_copy(row).start()
         own = dot_nn(synth_ref[half], mixed_ref[...])
-        scatter_rows(gather_f32, own_slot, own.shape[0], 2 * pair_rows, own)
+        scatter_rows(gather_own, own_slot, own.shape[0], pair_rows, own)
         high = dot_nn(synth_ref[2], mixed_ref[...])
         scatter_rows(gather_high, own_slot, high.shape[0], pair_rows, high)
 
-    def plane_pair(pair):
+    def pack(pair, first, source):
+        for block in range(blocks):
+            psend[pair, :, first : first + third, lanes_of(block)] = (
+                source[block].reshape(plane_count, third, lane_width).astype(jnp.bfloat16)
+            )
+
+    def start_plane(pair, side):
+        def one(step, carry):
+            p_copy(pair, side, step).start()
+            return carry
+
+        lax.fori_loop(1, plane_count, one, 0)
+
+    def own_pair(pair):
+        pack(pair, 0, gather_high)
+        pack(pair, third, gather_own)
+        start_plane(pair, 0)
+        precv[spot, pair, : 2 * third, :] = psend[pair, spot, : 2 * third, :]
+
+    def other_pair(pair):
         for inner in range(pair_rows):
             row = pair * pair_rows + inner
             z_copy(row).wait_recv()
             scatter_rows(
-                gather_f32,
-                pair_rows + inner,
-                zrecv.shape[1],
-                2 * pair_rows,
-                zrecv[row].astype(jnp.float32),
-            )
-        for block in range(blocks):
-            psend[pair, :, :low_piece, lanes_of(block)] = (
-                gather_f32[block, : plane_count * low_piece]
-                .reshape(plane_count, low_piece, lane_width)
-                .astype(jnp.bfloat16)
-            )
-            psend[pair, :, low_piece:, lanes_of(block)] = (
-                gather_high[block]
-                .reshape(plane_count, piece - low_piece, lane_width)
-                .astype(jnp.bfloat16)
-            )
-
+                gather_other, inner, zrecv.shape[1], pair_rows, zrecv[row].astype(jnp.float32)
+            )
+        pack(pair, 2 * third, gather_other)
+        start_plane(pair, 1)
+        precv[spot, pair, 2 * third :, :] = psend[pair, spot, 2 * third :, :]
+
+    group = pair_count * piece
+
+    def await_pair(pair, side):
         def one(step, carry):
-            p_copy(pair, step).start()
+            p_copy(pair, side, step).wait_recv()
             return carry
 
         lax.fori_loop(1, plane_count, one, 0)
-        precv[spot, pair] = psend[pair, spot]
-
-    group = pair_count * piece
-
-    def await_pair(pair):
-        def one(step, carry):
-            p_copy(pair, step).wait_recv()
-            return carry
-
-        lax.fori_loop(1, plane_count, one, 0)
+        begin, size = (0, 2 * third) if side == 0 else (2 * third, third)
 
         def widen(index, carry):
-            here = pl.ds(pl.multiple_of(index * group + pair * piece, piece), piece)
+            here = pl.ds(pl.multiple_of(index * group + pair * piece + begin, third), size)
             for block in range(blocks):
-                wave_f32[block, here, :] = precv[index, pair, :, lanes_of(block)].astype(
-                    jnp.float32
-                )
+                wave_f32[block, here, :] = precv[
+                    index, pair, begin : begin + size, lanes_of(block)
+                ].astype(jnp.float32)
             return carry
 
         lax.fori_loop(0, plane_count, widen, 0)
@@ -447,61 +479,86 @@
             axis=1,
         )
 
-    def send_chunk(chunk):
+    def start_return(index):
+        def one(step, carry):
+            r_copy(index, step).start()
+            return carry
+
+        lax.fori_loop(1, plane_count, one, 0)
+
+    def pack_return(slot, source):
         for block in range(blocks):
-            rsend[chunk, :, :, lanes_of(block)] = (
-                gather_f32[block].reshape(plane_count, piece, lane_width).astype(jnp.bfloat16)
-            )
-
+            rsend[slot, :, :, lanes_of(block)] = (
+                source[block].reshape(plane_count, piece, lane_width).astype(jnp.bfloat16)
+            )
+        rrecv[slot, spot] = rsend[slot, spot]
+
+    def await_return(index):
         def one(step, carry):
-            r_copy(chunk, step).start()
+            r_copy(index, step).wait_recv()
             return carry
 
         lax.fori_loop(1, plane_count, one, 0)
-        rrecv[chunk, spot] = rsend[chunk, spot]
-
-    def receive_chunk(chunk):
-        def one(step, carry):
-            r_copy(chunk, step).wait_recv()
-            return carry
-
-        lax.fori_loop(1, plane_count, one, 0)
-        for block in range(blocks):
-            gather_f32[block] = (
-                rrecv[chunk, :, :, lanes_of(block)]
-                .reshape(plane_count * piece, lane_width)
-                .astype(jnp.float32)
-            )
-
-    def low_chunk(chunk):
-        def one_order(inner, carry):
-            order = chunk * chunk_orders + inner
+
+    def low_analysis():
+        def one_order(order, carry):
             for phase in range(2):
                 key = order * 2 + phase
                 for side in range(2):
                     for row in range(row_count):
-                        slot = side * pair_rows + row % pair_rows
-                        first = (row // pair_rows) * piece + key * 2 * pair_rows + slot
+                        first = (row // pair_rows) * piece + (1 + side) * third
+                        first = first + key * pair_rows + row % pair_rows
                         collect(first, (side * row_count + row) * plane_count, phase)
             degree_grad = dot_nn(table_ref[order], wave_ref[...])
-            coeff_grad = mix((degree_grad * gain_low[:, 0:1]).astype(jnp.bfloat16))
-            lat_grad = dot_tn(table_ref[order], coeff_grad) * quad_ref[:, 0:1]
+            coeff_ref[order] = mix((degree_grad * gain_low[:, 0:1]).astype(jnp.bfloat16))
+            lat_grad = (
+                dot_tn(table_ref[order, :, own_lats:], coeff_ref[order]) * quad_ref[own_lats:, 0:1]
+            )
             for phase in range(2):
-                for slot in range(row_slots):
+                for row in range(row_count):
+                    first = (row // pair_rows) * third + (order * 2 + phase) * pair_rows
                     scatter_rows(
                         gather_f32,
-                        (inner * 2 + phase) * row_slots + slot,
+                        first + row % pair_rows,
                         plane_count,
                         piece,
                         lat_grad[
-                            slot * plane_count : (slot + 1) * plane_count,
+                            row * plane_count : (row + 1) * plane_count,
                             phase * channels : (phase + 1) * channels,
                         ],
                     )
             return carry
 
-        lax.fori_loop(0, chunk_orders, one_order, 0)
-        send_chunk(chunk)
+        lax.fori_loop(0, low_each, one_order, 0)
+        pack_return(0, gather_f32)
+        for pair in range(pair_count):
+            start_return(pair)
+
+    def scatter_own(target, key, lat_grad):
+        for phase in range(2):
+            for row in range(row_count):
+                scatter_rows(
+                    target,
+                    (key + phase) * row_count + row,
+                    plane_count,
+                    piece,
+                    lat_grad[
+                        row * plane_count : (row + 1) * plane_count,
+                        phase * channels : (phase + 1) * channels,
+                    ],
+                )
+
+    def low_own():
+        def one_order(order, carry):
+            lat_grad = (
+                dot_tn(table_ref[order, :, :own_lats], coeff_ref[order]) * quad_ref[:own_lats, 0:1]
+            )
+            scatter_own(gather_late, order * 2, lat_grad)
+            return carry
+
+        lax.fori_loop(0, low_each, one_order, 0)
+        pack_return(1, gather_late)
+        start_return(pair_count)
 
     high_first = [0, 5 * plane_count, 8 * plane_count, 4 * plane_count]
     high_size = [(high_each - slot) * plane_count for slot in range(high_each)]
@@ -511,12 +568,7 @@
             for phase in range(2):
                 key = slot * 2 + phase
                 for row in range(row_count):
-                    first = (
-                        (row // pair_rows) * piece
-                        + low_piece
-                        + key * pair_rows
-                        + row % pair_rows
-                    )
+                    first = (row // pair_rows) * piece + key * pair_rows + row % pair_rows
                     collect(first, row * plane_count, phase)
             here = slice(high_first[slot], high_first[slot] + high_size[slot])
             total = dot_nn(high_ref[slot, slot * plane_count :, :], wave_ref[:own_lats, :])
@@ -540,45 +592,44 @@
                 dot_tn(high_ref[slot, slot * plane_count :, :], high_coeff[here, :])
                 * quad_ref[:own_lats, 0:1]
             )
-            for phase in range(2):
-                for row in range(row_count):
-                    scatter_rows(
-                        gather_f32,
-                        (slot * 2 + phase) * row_count + row,
-                        plane_count,
-                        piece,
-                        lat_grad[
-                            row * plane_count : (row + 1) * plane_count,
-                            phase * channels : (phase + 1) * channels,
-                        ],
-                    )
-        send_chunk(low_chunks)
-
-    def return_low(chunk):
-        receive_chunk(chunk)
-        here = pl.ds(chunk * chunk_span, chunk_span)
+            scatter_own(gather_late, slot * 2, lat_grad)
+        pack_return(2, gather_late)
+        start_return(pair_count + 1)
+
+    def return_pair(pair):
+        await_return(pair)
+        begin = pair * third
+        for block in range(blocks):
+            gather_other[block] = (
+                rrecv[0, :, begin : begin + third, lanes_of(block)]
+                .reshape(plane_count * third, lane_width)
+                .astype(jnp.float32)
+            )
+        for inner in range(pair_rows):
+            for block in range(blocks):
+                zsend_back[pair * pair_rows + inner, :, lanes_of(block)] = gather_other[
+                    block, pl.ds(inner, zsend_back.shape[1], stride=pair_rows), :
+                ].astype(jnp.bfloat16)
+        zb_copy(pair).start()
+
+    def return_own(slot, target):
+        await_return(pair_count + slot - 1)
+        for block in range(blocks):
+            gather_f32[block] = (
+                rrecv[slot, :, :, lanes_of(block)]
+                .reshape(plane_count * piece, lane_width)
+                .astype(jnp.float32)
+            )
         for row in range(row_count):
             for block in range(blocks):
-                zsend_back[row, here, lanes_of(block)] = gather_f32[
-                    block, pl.ds(row_count + row, chunk_span, stride=row_slots), :
-                ].astype(jnp.bfloat16)
-        zb_copy(chunk).start()
-        for row in range(row_count):
-            for block in range(blocks):
-                yown[row, here, lanes_of(block)] = gather_f32[
-                    block, pl.ds(row, chunk_span, stride=row_slots), :
-                ].astype(jnp.bfloat16)
-
-    def return_high():
-        receive_chunk(low_chunks)
-        for row in range(row_count):
-            for block in range(blocks):
-                yhigh[row, :, lanes_of(block)] = gather_f32[
-                    block, pl.ds(row, yhigh.shape[1], stride=row_count), :
+                target[row, :, lanes_of(block)] = gather_f32[
+                    block, pl.ds(row, target.shape[1], stride=row_count), :
                 ].astype(jnp.bfloat16)
 
     forward_row(0)
     forward_row(1)
+    forward_row(2)
+    forward_row(3)
     for copy in local_copies:
         copy.wait()
     spread = lax.broadcasted_iota(jnp.int32, cosine_ref.shape, 0)
@@ -598,44 +649,49 @@
     )
     for row in range(row_count):
         loss_row(row)
-        if row + 2 < row_count:
-            forward_row(row + 2)
+        if row + 4 < row_count:
+            forward_row(row + 4)
         if row >= 1:
             backward_row(row - 1, (row - 1) % pair_rows)
             if row % pair_rows == 0:
-                plane_pair(row // pair_rows - 1)
+                own_pair(row // pair_rows - 1)
+            elif row > pair_rows:
+                other_pair(row // pair_rows - 1)
     backward_row(row_count - 1, (row_count - 1) % pair_rows)
+    own_pair(pair_count - 1)
     for pair in range(pair_count - 1):
-        await_pair(pair)
-    plane_pair(pair_count - 1)
-    await_pair(pair_count - 1)
-
+        await_pair(pair, 0)
+        await_pair(pair, 1)
+    other_pair(pair_count - 1)
+    await_pair(pair_count - 1, 0)
     high_analysis()
-    low_chunk(0)
+    await_pair(pair_count - 1, 1)
     high_middle()
-    for chunk in range(1, low_chunks):
-        low_chunk(chunk)
-        return_low(chunk - 1)
+    low_analysis()
     high_synthesis()
-    return_low(low_chunks - 1)
-    return_high()
+    for pair in range(pair_count):
+        return_pair(pair)
+    low_own()
+    return_own(2, yhigh)
+    return_own(1, yown)
 
     def own_part(row, carry):
         total_ref[row] = dot_nn(analysis_ref[half], yown[row]) + dot_nn(analysis_ref[2], yhigh[row])
         return carry
 
     lax.fori_loop(0, row_count, own_part, 0)
-    for chunk in range(low_chunks):
-        zb_copy(chunk).wait_recv()
 
     def finish(row, carry):
         spatial = total_ref[row] + dot_nn(analysis_ref[1 - half], zrecv_back[row])
-        out_ref[row] = (
+        saved_ref[row] = (
             cot_ref[row].astype(jnp.float32) + spatial * (1.0 / lon_count)
         ).astype(jnp.bfloat16)
+        out_copy(row).start()
         return carry
 
-    lax.fori_loop(0, row_count, finish, 0)
+    for pair in range(pair_count):
+        zb_copy(pair).wait_recv()
+        lax.fori_loop(pair * pair_rows, (pair + 1) * pair_rows, finish, 0)
 
     def drain_rows(row, carry):
         for step in range(1, member_count):
@@ -648,16 +704,19 @@
 
     def drain_plane(step, carry):
         for pair in range(pair_count):
-            p_copy(pair, step).wait_send()
-        for chunk in range(chunk_count):
-            r_copy(chunk, step).wait_send()
+            p_copy(pair, 0, step).wait_send()
+            p_copy(pair, 1, step).wait_send()
+        for index in range(pair_count + 2):
+            r_copy(index, step).wait_send()
         return carry
 
     lax.fori_loop(1, plane_count, drain_plane, 0)
-    for chunk in range(low_chunks):
-        zb_copy(chunk).wait_send()
+    for pair in range(pair_count):
+        zb_copy(pair).wait_send()
     high_copy().wait_send()
     coeff_copy().wait_send()
+    for row in range(row_count):
+        out_copy(row).wait()
 
 
 def shards(
@@ -670,10 +729,9 @@
     plane_count = lax.axis_size("lat") // 2
     part = lon_count // member_count
     pair_count = row_count // pair_rows
-    chunk_count = low_chunks + 1
     keys = plane_count * 2 * low_each
-    low_piece = 2 * low_each * 2 * pair_rows
-    piece = low_piece + 2 * high_each * pair_rows
+    third = 2 * low_each * pair_rows
+    piece = 3 * third
     order_slots = low_each + high_each
     region = (high_each + 1) * plane_count
     own_lats = row_count * plane_count
@@ -689,9 +747,13 @@
     result = pl.pallas_call(
         fused_kernel,
         out_shape=jax.ShapeDtypeStruct((row_count, lon_count, channels), bf16),
-        in_specs=[vmem, vmem, anywhere] + [vmem] * 7 + [anywhere] * 4,
-        out_specs=vmem,
+        in_specs=[anywhere] * 3 + [vmem] * 5 + [anywhere] * 6,
+        out_specs=anywhere,
         scratch_shapes=[
+            pltpu.VMEM((row_count, lon_count, channels), bf16),
+            pltpu.VMEM((row_count, lon_count, channels), bf16),
+            pltpu.VMEM(synth.shape, bf16),
+            pltpu.VMEM(analysis.shape, bf16),
             pltpu.VMEM((row_count, part, channels), bf16),
             pltpu.VMEM((order_slots, total_lat), f32),
             pltpu.VMEM((order_slots, total_lat), f32),
@@ -707,8 +769,11 @@
             pltpu.VMEM((row_count, lon_count, channels), bf16),
             pltpu.VMEM((row_count, lon_count, hidden), bf16),
             pltpu.VMEM((lon_count, channels), bf16),
+            pltpu.VMEM((blocks, plane_count * third, channels // blocks), f32),
+            pltpu.VMEM((blocks, plane_count * third, channels // blocks), f32),
+            pltpu.VMEM((blocks, plane_count * third, channels // blocks), f32),
             pltpu.VMEM((blocks, plane_count * piece, channels // blocks), f32),
-            pltpu.VMEM((blocks, plane_count * (piece - low_piece), channels // blocks), f32),
+            pltpu.VMEM((blocks, plane_count * piece, channels // blocks), f32),
             pltpu.VMEM((row_count, keys, channels), bf16),
             pltpu.VMEM((row_count, keys, channels), bf16),
             pltpu.VMEM((pair_count, plane_count, piece, channels), bf16),
@@ -718,30 +783,32 @@
             pltpu.VMEM((low_each, total_lat, total_lat), bf16),
             pltpu.VMEM((high_each, high_each * plane_count, own_lats), bf16),
             pltpu.VMEM((total_lat, 2 * channels), bf16),
+            pltpu.VMEM((low_each, total_lat, 2 * channels), bf16),
             pltpu.VMEM((2 * region, 2 * channels), f32),
             pltpu.VMEM((2 * region, 2 * channels), bf16),
             pltpu.VMEM((region, 2 * channels), bf16),
             pltpu.VMEM((2 * region, 2 * channels), bf16),
             pltpu.VMEM((row_count, lon_count, channels), f32),
-            pltpu.VMEM((chunk_count, plane_count, piece, channels), bf16),
-            pltpu.VMEM((chunk_count, plane_count, piece, channels), bf16),
+            pltpu.VMEM((3, plane_count, piece, channels), bf16),
+            pltpu.VMEM((3, plane_count, piece, channels), bf16),
             pltpu.VMEM((row_count, keys, channels), bf16),
             pltpu.VMEM((row_count, keys, channels), bf16),
             pltpu.VMEM((row_count, keys, channels), bf16),
             pltpu.VMEM((row_count, keys, channels), bf16),
-            dma((5,)),
+            dma((7,)),
+            dma((3, row_count)),
             dma((row_count, member_count - 1)),
             dma((row_count, member_count - 1)),
             dma((row_count, member_count - 1)),
             dma((row_count, member_count - 1)),
             dma((row_count,)),
             dma((row_count,)),
-            dma((pair_count, plane_count)),
-            dma((pair_count, plane_count)),
-            dma((chunk_count, plane_count)),
-            dma((chunk_count, plane_count)),
-            dma((low_chunks,)),
-            dma((low_chunks,)),
+            dma((pair_count, 2, plane_count)),
+            dma((pair_count, 2, plane_count)),
+            dma((pair_count + 2, plane_count)),
+            dma((pair_count + 2, plane_count)),
+            dma((pair_count,)),
+            dma((pair_count,)),
             dma((2,)),
             dma((2,)),
         ],

time: 231 us -> 227 us (0.983); the launches traced: 229 us -> 223 us
  Pallas kernels: 225 us -> 218 us
    pallas_call x1, Pallas kernels: 225 us -> 218 us  [shards(): pl.pallas_call(fused_kernel, out_shape=jax.ShapeDtypeStruct((row_count, l...]
where the time goes in v4:
time: 227 us; the launch traced here: 223 us
  Pallas kernels  218 us (96%)
  local copies, waits for them, and re-layouts  4.47 us (2%)
    pallas_call x1, Pallas kernels, shards(): pl.pallas_call(fused_kernel, out_shape=jax.ShapeDtypeStruct((row_count, l...  218 us

profile of v4, /device:TPU:102, one launch (start us, length us, event | category | flops | bytes accessed | tf_op | source)
XLA Modules:
  0.0 222.7 jit_solution(15882216957648125355)
XLA Ops:
  0.0 1.2 broadcast_in_dim.6.gain_ref
  1.2 218.2 %shard_map.136 = bf16[6,768,256]{2,1,0:T(8,128)(2,1)} custom-call(bf16[6,768,256]{2,1,0:T(8,128)(2,1)} %bitcast.4, bf16[6,768,256]{2,1,0:T(8,128)(2,1)} %bitcast.5, bf16[6,768,256]{2,1,0:T(8,128)(2,1)} %target_ref.1, s32[6,768]{1,0:T(8,128)} %land_ref.1, bf16[256,256]{1,0:T(8,128)(2,1)} %mix_ref.1, f32[1,384]{1,0:T(1,128)} %broadcast_in_dim.6.gain_ref, ...), custom_call_target="tpu_custom_call" | custom-call | tf_op jit(solution)/shard_map/pallas_call | solution.py:747
  219.5 3.2 %copy.16 = bf16[1,6,768,256]{3,2,1,0:T(8,128)(2,1)} copy(bf16[1,6,768,256]{3,2,1,0:T(8,128)(2,1)} %bitcast.3) | data formatting | bytes 4718592

commit v5 on v4

--- a/solution.py
+++ b/solution.py
@@ -639,7 +639,7 @@
     weight_rows[...] = jnp.zeros(weight_rows.shape, jnp.float32)
     weight_rows[:row_count, :] = land_ref[...].astype(jnp.float32) * area_ref[:row_count, 0:1]
     weight_ref[...] = weight_rows[...].T
-    gain_low[...] = jnp.broadcast_to(gain_ref[...], (8, total_lat)).T
+    gain_low[...] = jnp.broadcast_to(gain_ref[...][None, :], (8, total_lat)).T
     for slot in range(high_each):
         gain_high[high_first[slot] : high_first[slot] + high_size[slot], :] = gain_low[
             total_lat - high_size[slot] :, :
@@ -821,7 +821,7 @@
         target,
         land_weight,
         mix_weight,
-        degree_gain[None, :],
+        degree_gain,
         up_weight,
         down_weight,
         synth,

time: 227 us -> 225 us (level)
  no operation moved by 1% of the time
where the time goes in v5:
time: 225 us; the launch traced here: 221 us
  Pallas kernels  218 us (97%)
  local copies, waits for them, and re-layouts  3.22 us (1%)
    pallas_call x1, Pallas kernels, shards(): pl.pallas_call(fused_kernel, out_shape=jax.ShapeDtypeStruct((row_count, l...  218 us

profile of v5, /device:TPU:102, one launch (start us, length us, event | category | flops | bytes accessed | tf_op | source)
XLA Modules:
  0.0 221.0 jit_solution(13980473477801730125)
XLA Ops:
  0.0 217.7 %shard_map.136 = bf16[6,768,256]{2,1,0:T(8,128)(2,1)} custom-call(bf16[6,768,256]{2,1,0:T(8,128)(2,1)} %bitcast.4, bf16[6,768,256]{2,1,0:T(8,128)(2,1)} %bitcast.5, bf16[6,768,256]{2,1,0:T(8,128)(2,1)} %target_ref.1, s32[6,768]{1,0:T(8,128)} %land_ref.1, bf16[256,256]{1,0:T(8,128)(2,1)} %mix_ref.1, f32[384]{0:T(512)} %gain_ref.1, bf16[256,512]{1,0:T(8,128)(2,1)} %up_ref.1, ...), custom_call_target="tpu_custom_call" | custom-call | tf_op jit(solution)/shard_map/pallas_call | solution.py:747
  217.7 3.2 %copy.16 = bf16[1,6,768,256]{3,2,1,0:T(8,128)(2,1)} copy(bf16[1,6,768,256]{3,2,1,0:T(8,128)(2,1)} %bitcast.3) | data formatting | bytes 4718592
